TPU v7x, 256 devices: a whole 4x4x8 slice. The times are simulated.
256 devices in a mesh: fsdp: 32 (over x, z), rep: 8 (over y, core).
Axes of the slice: x: 4, y: 4, z: 8, core: 2. Of those that a mesh axis runs over, the one named last changes fastest.
Arguments:
- grads: bfloat16 [8, 1024, 28672], P('rep', 'fsdp'), may hold values from -5 to 5
- owner: int32 [2, 56], replicated, may hold values from 0 to 31, as said below
- left_stats: float32 [8, 32, 2, 512, 512], P('rep', 'fsdp'), may hold values from -0.12 to 4, as said below
- right_stats: float32 [8, 32, 2, 512, 512], P('rep', 'fsdp'), may hold values from -0.12 to 4, as said below
- left_root: bfloat16 [8, 32, 2, 512, 512], P('rep', 'fsdp'), may hold values from -0.2 to 1.5, as said below
- right_root: bfloat16 [8, 32, 2, 512, 512], P('rep', 'fsdp'), may hold values from -0.2 to 1.5, as said below
Outputs:
- update: bfloat16 [1024, 28672], P('fsdp', 'rep')
- new_left: float32 [8, 32, 2, 512, 512], P('rep', 'fsdp')
- new_right: float32 [8, 32, 2, 512, 512], P('rep', 'fsdp')
Inputs may be any that keep to these rules, and one draw needn't show every extreme that they name: In each block row the 7 block columns of one group (columns r * 7 to (r + 1) * 7 - 1) have distinct owners; in every group some owner holds a block in every block row. `left_stats`: each slot is symmetric. `right_stats`: each slot is symmetric. `left_root`: each slot is symmetric. `right_root`: each slot is symmetric.
All inputs are finite; a program needn't handle non-finite values.
Results may differ from a plain program's by a relative error of at most 0.022.
Values may be sent and summed in bfloat16 or wider, within the bound.
No kernel may reach another device: no remote copies, remote signals or barrier semaphores. Data moves between devices by JAX's collectives and lax.ppermute only.
A program may use at most 64 MiB of HBM per device.

v0:
```python
import jax
import jax.numpy as jnp
from jax import lax
from jax.sharding import PartitionSpec as P

BETA = 0.9
EPS = 1e-06


def precondition(g, left, right, lroot, rroot):
    block = g.shape[0]
    gram_left = (
        lax.dot_general(g, g, (((1,), (1,)), ((), ())), preferred_element_type=jnp.float32) / block
    )
    gram_right = (
        lax.dot_general(g, g, (((0,), (0,)), ((), ())), preferred_element_type=jnp.float32) / block
    )
    new_left = BETA * left + gram_left
    new_right = BETA * right + gram_right
    half = jnp.dot(lroot, g, preferred_element_type=jnp.float32).astype(jnp.bfloat16)
    pre = jnp.dot(half, rroot, preferred_element_type=jnp.float32)
    gfull = g.astype(jnp.float32)
    scale = jnp.sqrt(jnp.mean(gfull * gfull)) / jnp.sqrt(jnp.mean(pre * pre) + EPS)
    return ((scale * pre).astype(jnp.bfloat16), new_left, new_right)


def on_device(grads, owner, left_stats, right_stats, left_root, right_root):
    strip = grads.shape[1]
    n_fsdp = lax.axis_size("fsdp")
    n_rep = lax.axis_size("rep")
    block = left_stats.shape[-1]
    slots = left_stats.shape[2]
    width = grads.shape[2] // n_rep
    group_list = width // block
    rep_index = lax.axis_index("rep")
    fsdp_index = lax.axis_index("fsdp")
    shard = grads[0].astype(jnp.float32)
    summed = lax.psum(shard.astype(jnp.bfloat16), "rep").astype(jnp.float32)
    mine = lax.dynamic_slice_in_dim(summed, rep_index * width, width, 1)
    grad_part = mine.astype(jnp.bfloat16)
    block_row = fsdp_index * strip // block
    owner_row = lax.dynamic_index_in_dim(owner, block_row, 0, keepdims=False)
    owner_cols = lax.dynamic_slice_in_dim(owner_row, rep_index * group_list, group_list, 0)
    select = (jnp.arange(n_fsdp, dtype=jnp.int32)[:, None] == owner_cols[None, :]).astype(
        jnp.bfloat16
    )
    pieces = grad_part.reshape(strip, group_list, block)
    outgoing = jnp.einsum("oc,scd->osd", select, pieces, preferred_element_type=jnp.float32).astype(
        jnp.bfloat16
    )
    incoming = lax.all_to_all(outgoing, "fsdp", split_axis=0, concat_axis=0, tiled=True)
    block_list = incoming.reshape(slots, block, block)
    lefts = left_stats[0, 0]
    rights = right_stats[0, 0]
    lroots = left_root[0, 0]
    rroots = right_root[0, 0]
    results, new_l, new_r = jax.vmap(precondition)(block_list, lefts, rights, lroots, rroots)
    going_back = results.reshape(n_fsdp, strip, block)
    returned = lax.all_to_all(going_back, "fsdp", split_axis=0, concat_axis=0, tiled=True)
    placed = jnp.einsum("oc,osd->scd", select, returned, preferred_element_type=jnp.float32).astype(
        jnp.bfloat16
    )
    update = placed.reshape(strip, width)
    return (update, new_l[None, None], new_r[None, None])


def solution(mesh):
    in_specs = (
        P("rep", "fsdp", None),
        P(),
        P("rep", "fsdp", None, None, None),
        P("rep", "fsdp", None, None, None),
        P("rep", "fsdp", None, None, None),
        P("rep", "fsdp", None, None, None),
    )
    out_specs = (
        P("fsdp", "rep"),
        P("rep", "fsdp", None, None, None),
        P("rep", "fsdp", None, None, None),
    )
    return jax.shard_map(
        on_device, mesh=mesh, in_specs=in_specs, out_specs=out_specs, check_vma=False
    )
```

profile of v0, /device:TPU:24, one launch (start us, length us, event | category | flops | bytes accessed | tf_op | source)
XLA Modules:
  0.0 171.6 jit_solution(4918326397261587423)
XLA Ops:
  7.2 0.0 copy-start
  7.2 0.0 all-reduce.2.cloned.1.call-start
  7.2 0.7 all-reduce.2.cloned.1.call-update
  7.9 0.8 dynamic-slice_bitcast_fusion
  8.7 72.0 %all-reduce.2.cloned.1.call-done = bf16[32,28672]{1,0:T(8,128)(2,1)} async-done(((bf16[32,28672]{1,0:T(8,128)(2,1)}), bf16[32,28672]{1,0:T(8,128)(2,1)}) %all-reduce.2.cloned.1.call-update) | async-done | bytes 1835024 | tf_op jit(solution)/shard_map/psum | solution.py:38
  80.7 1.0 convert_convert_fusion
  81.6 0.3 reshape.35
  81.9 0.6 convolution_convert_fusion.1
  82.5 0.6 copy.14
  83.1 0.0 copy-start.2
  83.1 38.4 %all_to_all.10 = bf16[32,32,512]{2,1,0:T(8,128)(2,1)S(1)} all-to-all(bf16[32,32,512]{2,1,0:T(8,128)(2,1)S(1)} %copy.14), channel_id=1, replica_groups=mesh['fsdp'=32,'rep'=8] {'fsdp'}, dimensions={0} | all-to-all | bytes 2097152 | tf_op jit(solution)/shard_map/all_to_all | solution.py:51
  121.5 0.4 multiply_reduce_fusion.1
  121.9 0.1 reduce_sum.26
  122.0 0.1 reduce_sum.27
  122.1 0.0 copy-done
  122.1 0.0 copy-done.2
  122.1 2.8 %multiply_reduce_fusion = (f32[2]{0:T(128)S(1)}, f32[2,512,512]{2,1,0:T(8,128)}) fusion(bf16[1,1,2,512,512]{4,3,2,1,0:T(8,128)(2,1)S(1)} %copy-done, bf16[2,512,512]{2,1,0:T(8,128)(2,1)S(1)} %bitcast.41, bf16[1,1,2,512,512]{4,3,2,1,0:T(8,128)(2,1)S(1)} %copy-done.2), kind=kOutput, calls=%fused_computation.5 | convolution fusion | flops 1075314688 | bytes 5242888 | tf_op jit(solution)/shard_map/vmap()/dot_general | solution.py:21
  124.9 2.9 %multiply_convert_fusion = bf16[2,512,512]{2,1,0:T(8,128)(2,1)} fusion(f32[2,512,512]{2,1,0:T(8,128)} %get-tuple-element.4, f32[2]{0:T(128)S(1)} %rsqrt_multiply_fusion), kind=kLoop, calls=%fused_computation.4 | loop fusion | flops 1048576 | bytes 3145736 | tf_op jit(solution)/shard_map/vmap()/convert_element_type | solution.py:24
  127.8 6.6 %all-to-all-start.1 = ((bf16[32,32,512]{2,1,0:T(8,128)(2,1)}), bf16[32,32,512]{2,1,0:T(8,128)(2,1)S(1)}, u32[]{:S(2)}, u32[]{:S(2)}) async-start(bf16[32,32,512]{2,1,0:T(8,128)(2,1)} %bitcast.6), calls=%async_computation.1 | async-start | bytes 2097152 | tf_op jit(solution)/shard_map/all_to_all | solution.py:59
  134.4 0.0 copy-start.1
  134.4 3.9 %fusion = f32[1,1,2,512,512]{4,3,2,1,0:T(8,128)} fusion(f32[1,1,2,512,512]{4,3,2,1,0:T(8,128)} %param.9, bf16[2,512,512]{2,1,0:T(8,128)(2,1)S(1)} %bitcast.42), kind=kOutput, calls=%fused_computation.1 | convolution fusion | flops 538443776 | bytes 5242880 | tf_op jit(solution)/shard_map/vmap()/dot_general | solution.py:16
  138.3 0.0 copy-done.1
  138.3 2.1 %fusion.1 = f32[1,1,2,512,512]{4,3,2,1,0:T(8,128)} fusion(f32[1,1,2,512,512]{4,3,2,1,0:T(8,128)S(1)} %copy-done.1, bf16[2,512,512]{2,1,0:T(8,128)(2,1)S(1)} %bitcast.43), kind=kOutput, calls=%fused_computation.3 | convolution fusion | flops 538443776 | bytes 5242880 | tf_op jit(solution)/shard_map/vmap()/dot_general | solution.py:13
  140.4 22.9 %all-to-all-done.1 = bf16[32,32,512]{2,1,0:T(8,128)(2,1)S(1)} async-done(((bf16[32,32,512]{2,1,0:T(8,128)(2,1)}), bf16[32,32,512]{2,1,0:T(8,128)(2,1)S(1)}, u32[]{:S(2)}, u32[]{:S(2)}) %all-to-all-start.1) | async-done | bytes 1048608 | tf_op jit(solution)/shard_map/all_to_all | solution.py:59
  163.3 0.7 convolution_convert_fusion.2
  163.9 0.8 copy.22
  (1 shorter events, 0.0 us)
Async XLA Ops:
  7.2 114.9 %copy-start = (bf16[1,1,2,512,512]{4,3,2,1,0:T(8,128)(2,1)S(1)}, bf16[1,1,2,512,512]{4,3,2,1,0:T(8,128)(2,1)}, u32[]{:S(2)}) copy-start(bf16[1,1,2,512,512]{4,3,2,1,0:T(8,128)(2,1)} %param.11) | copy-start | bytes 3145732
  7.2 73.5 %all-reduce.2.cloned.1.call-start = ((), (), s32[]{:S(2)}) async-start(), calls=%async_computation.2 | async-start | bytes 3670016 | tf_op jit(solution)/shard_map/psum | solution.py:38
  83.1 39.0 %copy-start.2 = (bf16[1,1,2,512,512]{4,3,2,1,0:T(8,128)(2,1)S(1)}, bf16[1,1,2,512,512]{4,3,2,1,0:T(8,128)(2,1)}, u32[]{:S(2)}) copy-start(bf16[1,1,2,512,512]{4,3,2,1,0:T(8,128)(2,1)} %param.10) | copy-start | bytes 3145732
  127.8 35.5 %all-to-all-start.1 = ((bf16[32,32,512]{2,1,0:T(8,128)(2,1)}), bf16[32,32,512]{2,1,0:T(8,128)(2,1)S(1)}, u32[]{:S(2)}, u32[]{:S(2)}) async-start(bf16[32,32,512]{2,1,0:T(8,128)(2,1)} %bitcast.6), calls=%async_computation.1 | async-start | bytes 2097152 | tf_op jit(solution)/shard_map/all_to_all | solution.py:59
  134.4 3.9 %copy-start.1 = (f32[1,1,2,512,512]{4,3,2,1,0:T(8,128)S(1)}, f32[1,1,2,512,512]{4,3,2,1,0:T(8,128)}, u32[]{:S(2)}) copy-start(f32[1,1,2,512,512]{4,3,2,1,0:T(8,128)} %param.8) | copy-start | bytes 6291460
Sparse Core Ops, SparseCore 0:
  10.4 70.2 all-reduce.1
where the time goes:
time: 172 us
  waiting for transfers between devices  95.5 us (56%)
  blocking collectives  38.4 us (22%)
  between operations  14.1 us (8%)
  matrix products  10 us (6%)
  starting transfers between devices  6.61 us (4%)
  other arithmetic  4.35 us (3%)
  local copies, waits for them, and re-layouts  2.5 us (1%)
    psum x1, waiting for transfers between devices, on_device(): summed = lax.psum(shard.astype(jnp.bfloat16), 'rep').astype(jnp.float32)  72 us
    all_to_all x1, blocking collectives, on_device(): lax.all_to_all(outgoing, 'fsdp', split_axis=0, concat_axis=0, tiled=True)  38.4 us
    all_to_all x1, waiting for transfers between devices, on_device(): lax.all_to_all(going_back, 'fsdp', split_axis=0, concat_axis=0, tiled=True)  22.9 us
    all_to_all x1, starting transfers between devices, on_device(): lax.all_to_all(going_back, 'fsdp', split_axis=0, concat_axis=0, tiled=True)  6.57 us
    dot_general x1, matrix products, precondition(): lax.dot_general(g, g, (((0,), (0,)), ((), ())), preferred_element_type=jn...  3.9 us
  transfers between devices with their start and end apart: 2, of which 2 were waited for; matrix products, arithmetic and copies ran while one was open for 4% of the time, Pallas kernels for 0%

commit v1 on v0

--- a/solution.py
+++ b/solution.py
@@ -24,6 +24,37 @@
     return ((scale * pre).astype(jnp.bfloat16), new_left, new_right)
 
 
+def sum_over_rep(shard, width):
+    n_rep = lax.axis_size("rep")
+    rep_index = lax.axis_index("rep")
+    core = rep_index % 2
+    ring = n_rep // 2
+    y_index = rep_index // 2
+
+    def group(array, index):
+        return lax.dynamic_slice_in_dim(array, index * width, width, 1)
+
+    sent = jnp.concatenate([group(shard, 2 * i + 1 - core) for i in range(ring)], axis=1)
+    other = lax.ppermute(sent, "rep", [(i, i + 1 - 2 * (i % 2)) for i in range(n_rep)])
+    parts = []
+    for step in range(ring):
+        target = (y_index + step) % ring
+        mine = group(shard, 2 * target + core).astype(jnp.float32)
+        parts.append(mine + group(other, target).astype(jnp.float32))
+    total = parts[0]
+    arrived = [
+        lax.ppermute(
+            parts[step].astype(jnp.bfloat16),
+            "rep",
+            [(i, (i + 2 * step) % n_rep) for i in range(n_rep)],
+        )
+        for step in range(1, ring)
+    ]
+    for part in arrived:
+        total = total + part.astype(jnp.float32)
+    return total.astype(jnp.bfloat16)
+
+
 def on_device(grads, owner, left_stats, right_stats, left_root, right_root):
     strip = grads.shape[1]
     n_fsdp = lax.axis_size("fsdp")
@@ -34,10 +65,7 @@
     group_list = width // block
     rep_index = lax.axis_index("rep")
     fsdp_index = lax.axis_index("fsdp")
-    shard = grads[0].astype(jnp.float32)
-    summed = lax.psum(shard.astype(jnp.bfloat16), "rep").astype(jnp.float32)
-    mine = lax.dynamic_slice_in_dim(summed, rep_index * width, width, 1)
-    grad_part = mine.astype(jnp.bfloat16)
+    grad_part = sum_over_rep(grads[0], width)
     block_row = fsdp_index * strip // block
     owner_row = lax.dynamic_index_in_dim(owner, block_row, 0, keepdims=False)
     owner_cols = lax.dynamic_slice_in_dim(owner_row, rep_index * group_list, group_list, 0)

time: 172 us -> 107 us (0.62)
  the two profiles are of different devices: /device:TPU:24 before, /device:TPU:32 now
where the time goes in v1:
time: 107 us; the launch traced here: 106 us
  blocking collectives  39.2 us (37%)
  waiting for transfers between devices  34.3 us (32%)
  starting transfers between devices  11 us (10%)
  matrix products  9.95 us (9%)
  other arithmetic  7.79 us (7%)
  local copies, waits for them, and re-layouts  3.31 us (3%)
    all_to_all x1, blocking collectives, on_device(): lax.all_to_all(outgoing, 'fsdp', split_axis=0, concat_axis=0, tiled=True)  39.2 us
    all_to_all x1, waiting for transfers between devices, on_device(): lax.all_to_all(going_back, 'fsdp', split_axis=0, concat_axis=0, tiled=True)  22.1 us
    ppermute x3, waiting for transfers between devices, sum_over_rep(): lax.ppermute(parts[step].astype(jnp.bfloat16), 'rep', [(i, (i + 2 * step)...  9.45 us
    ppermute x3, starting transfers between devices, sum_over_rep(): lax.ppermute(parts[step].astype(jnp.bfloat16), 'rep', [(i, (i + 2 * step)...  5.83 us
    all_to_all x1, starting transfers between devices, on_device(): lax.all_to_all(going_back, 'fsdp', split_axis=0, concat_axis=0, tiled=True)  5.19 us
    dot_general x1, matrix products, precondition(): lax.dot_general(g, g, (((0,), (0,)), ((), ())), preferred_element_type=jn...  3.88 us
    convert_element_type x1, other arithmetic, precondition(): return ((scale * pre).astype(jnp.bfloat16), new_left, new_right)  2.88 us
    ppermute x1, waiting for transfers between devices, sum_over_rep(): lax.ppermute(sent, 'rep', [(i, i + 1 - 2 * (i % 2)) for i in range(n_rep)])  2.81 us
  transfers between devices with their start and end apart: 5, of which 4 were waited for; matrix products, arithmetic and copies ran while one was open for 6% of the time, Pallas kernels for 0%

profile of v1, /device:TPU:32, one launch (start us, length us, event | category | flops | bytes accessed | tf_op | source)
XLA Modules:
  0.0 106.3 jit_solution(7504821230706304577)
XLA Ops:
  0.6 0.0 copy-start
  0.6 0.0 copy-start.2
  0.7 1.5 %dynamic-slice_bitcast_fusion.3 = (bf16[32,3584]{1,0:T(8,128)(2,1)S(1)}, bf16[32,3584]{1,0:T(8,128)(2,1)S(1)}, bf16[32,3584]{1,0:T(8,128)(2,1)S(1)}, bf16[32,3584]{1,0:T(8,128)(2,1)S(1)}) fusion(bf16[1,32,28672]{2,1,0:T(8,128)(2,1)} %param.6, s32[]{:T(128)S(6)} %select_n.86, s32[]{:T(128)S(6)} %select_n.89, s32[]{:T(128)S(6)} %select_n.88, s32[]{:T(128)S(6)} %select_n.87), kind=kLoop, calls=%fused_computation.29 | loop fusion | bytes 1835024 | tf_op jit(solution)/shard_map/dynamic_slice | solution.py:35
  2.2 0.0 copy-start.3
  2.2 1.0 pad_maximum_fusion
  3.2 0.0 collective-permute-start
  3.2 2.8 %collective-permute-done = bf16[32,14336]{1,0:T(8,128)(2,1)} collective-permute-done((bf16[32,14336]{1,0:T(8,128)(2,1)}, bf16[32,14336]{1,0:T(8,128)(2,1)}, u32[]{:S(2)}, u32[]{:S(2)}) %collective-permute-start) | collective-permute-done | bytes 917536 | tf_op jit(solution)/shard_map/ppermute | solution.py:38
  6.0 0.0 copy-done.2
  6.0 2.0 %fusion.9 = (bf16[32,3584]{1,0:T(8,128)(2,1)}, bf16[32,3584]{1,0:T(8,128)(2,1)S(1)}, bf16[32,3584]{1,0:T(8,128)(2,1)S(1)}) fusion(bf16[32,14336]{1,0:T(8,128)(2,1)} %collective-permute-done, s32[]{:T(128)S(6)} %select_n.93, bf16[1,32,28672]{2,1,0:T(8,128)(2,1)S(1)} %copy-done.2, s32[]{:T(128)S(6)} %select_n.92, s32[]{:T(128)S(6)} %select_n.99, ...), kind=kLoop, calls=%fused_computation.20 | loop fusion | flops 1376256 | bytes 2064408 | tf_op jit(solution)/shard_map/convert_element_type | solution.py:47
  8.0 1.6 %collective-permute-start.1 = (bf16[32,3584]{1,0:T(8,128)(2,1)}, bf16[32,3584]{1,0:T(8,128)(2,1)}, u32[]{:S(2)}, u32[]{:S(2)}) collective-permute-start(bf16[32,3584]{1,0:T(8,128)(2,1)} %get-tuple-element.3), channel_id=1, source_target_pairs={{0,2},{1,3},{2,4},{3,5},{4,6},{5,7},{6,0},{7,1},{8,10},{9,11},{10,... | collective-permute-start | bytes 688136 | tf_op jit(solution)/shard_map/ppermute | solution.py:46
  9.6 2.9 %collective-permute-start.2 = (bf16[32,3584]{1,0:T(8,128)(2,1)S(1)}, bf16[32,3584]{1,0:T(8,128)(2,1)}, u32[]{:S(2)}, u32[]{:S(2)}) collective-permute-start(bf16[32,3584]{1,0:T(8,128)(2,1)S(1)} %get-tuple-element.5), channel_id=1, source_target_pairs={{0,4},{1,5},{2,6},{3,7},{4,0},{5,1},{6,2},{7,3},{8,12},{9,13},{10,... | collective-permute-start | bytes 688136 | tf_op jit(solution)/shard_map/ppermute | solution.py:46
  12.5 1.3 %collective-permute-start.3 = (bf16[32,3584]{1,0:T(8,128)(2,1)S(1)}, bf16[32,3584]{1,0:T(8,128)(2,1)}, u32[]{:S(2)}, u32[]{:S(2)}) collective-permute-start(bf16[32,3584]{1,0:T(8,128)(2,1)S(1)} %get-tuple-element.4), channel_id=1, source_target_pairs={{0,6},{1,7},{2,0},{3,1},{4,2},{5,3},{6,4},{7,5},{8,14},{9,15},{10,... | collective-permute-start | bytes 688136 | tf_op jit(solution)/shard_map/ppermute | solution.py:46
  13.8 0.0 copy-done.3
  13.8 0.1 dynamic-slice_bitcast_fusion.4
  13.9 3.4 %collective-permute-done.1 = bf16[32,3584]{1,0:T(8,128)(2,1)} collective-permute-done((bf16[32,3584]{1,0:T(8,128)(2,1)}, bf16[32,3584]{1,0:T(8,128)(2,1)}, u32[]{:S(2)}, u32[]{:S(2)}) %collective-permute-start.1) | collective-permute-done | bytes 229408 | tf_op jit(solution)/shard_map/ppermute | solution.py:46
  17.2 6.1 %collective-permute-done.2 = bf16[32,3584]{1,0:T(8,128)(2,1)} collective-permute-done((bf16[32,3584]{1,0:T(8,128)(2,1)S(1)}, bf16[32,3584]{1,0:T(8,128)(2,1)}, u32[]{:S(2)}, u32[]{:S(2)}) %collective-permute-start.2) | collective-permute-done | bytes 229408 | tf_op jit(solution)/shard_map/ppermute | solution.py:46
  23.3 0.0 collective-permute-done.3
  23.3 1.4 %fusion.13 = bf16[32,3584]{1,0:T(8,128)(2,1)S(1)} fusion(bf16[32,3584]{1,0:T(8,128)(2,1)} %collective-permute-done.3, bf16[32,3584]{1,0:T(8,128)(2,1)} %collective-permute-done.2, bf16[32,3584]{1,0:T(8,128)(2,1)} %collective-permute-done.1, bf16[32,14336]{1,0:T(8,128)(2,1)} %collective-permute-done, s32[]{:T(128)S(6)} %select_n.90, ...), kind=kLoop, calls=%fused_computation.25 | loop fusion | flops 1146880 | bytes 1376264 | tf_op jit(solution)/shard_map/convert_element_type | solution.py:55
  24.8 0.3 reshape.51
  25.1 0.6 convolution_convert_fusion.1
  25.6 0.6 copy.14
  26.2 0.0 copy-start.4
  26.2 39.2 %all_to_all.10 = bf16[32,32,512]{2,1,0:T(8,128)(2,1)S(1)} all-to-all(bf16[32,32,512]{2,1,0:T(8,128)(2,1)S(1)} %copy.14), channel_id=1, replica_groups=mesh['fsdp'=32,'rep'=8] {'fsdp'}, dimensions={0} | all-to-all | bytes 2097152 | tf_op jit(solution)/shard_map/all_to_all | solution.py:79
  65.4 0.4 multiply_reduce_fusion.1
  65.8 0.1 reduce_sum.26
  65.9 0.1 reduce_sum.27
  66.0 0.0 copy-done
  66.0 0.0 copy-done.4
  66.0 2.8 %multiply_reduce_fusion = (f32[2]{0:T(128)S(1)}, f32[2,512,512]{2,1,0:T(8,128)}) fusion(bf16[1,1,2,512,512]{4,3,2,1,0:T(8,128)(2,1)S(1)} %copy-done, bf16[2,512,512]{2,1,0:T(8,128)(2,1)S(1)} %bitcast.60, bf16[1,1,2,512,512]{4,3,2,1,0:T(8,128)(2,1)S(1)} %copy-done.4), kind=kOutput, calls=%fused_computation.5 | convolution fusion | flops 1075314688 | bytes 5242888 | tf_op jit(solution)/shard_map/vmap()/dot_general | solution.py:21
  68.8 2.9 %multiply_convert_fusion = bf16[2,512,512]{2,1,0:T(8,128)(2,1)} fusion(f32[2,512,512]{2,1,0:T(8,128)} %get-tuple-element.11, f32[2]{0:T(128)S(1)} %rsqrt_multiply_fusion), kind=kLoop, calls=%fused_computation.4 | loop fusion | flops 1048576 | bytes 3145736 | tf_op jit(solution)/shard_map/vmap()/convert_element_type | solution.py:24
  71.6 5.2 %all-to-all-start.1 = ((bf16[32,32,512]{2,1,0:T(8,128)(2,1)}), bf16[32,32,512]{2,1,0:T(8,128)(2,1)S(1)}, u32[]{:S(2)}, u32[]{:S(2)}) async-start(bf16[32,32,512]{2,1,0:T(8,128)(2,1)} %bitcast.13), calls=%async_computation.1 | async-start | bytes 2097152 | tf_op jit(solution)/shard_map/all_to_all | solution.py:87
  76.8 0.0 copy-start.1
  76.9 3.9 %fusion = f32[1,1,2,512,512]{4,3,2,1,0:T(8,128)} fusion(f32[1,1,2,512,512]{4,3,2,1,0:T(8,128)} %param.9, bf16[2,512,512]{2,1,0:T(8,128)(2,1)S(1)} %bitcast.61), kind=kOutput, calls=%fused_computation.1 | convolution fusion | flops 538443776 | bytes 5242880 | tf_op jit(solution)/shard_map/vmap()/dot_general | solution.py:16
  80.7 0.0 copy-done.1
  80.7 2.1 %fusion.1 = f32[1,1,2,512,512]{4,3,2,1,0:T(8,128)} fusion(f32[1,1,2,512,512]{4,3,2,1,0:T(8,128)S(1)} %copy-done.1, bf16[2,512,512]{2,1,0:T(8,128)(2,1)S(1)} %bitcast.62), kind=kOutput, calls=%fused_computation.3 | convolution fusion | flops 538443776 | bytes 5242880 | tf_op jit(solution)/shard_map/vmap()/dot_general | solution.py:13
  82.8 22.1 %all-to-all-done.1 = bf16[32,32,512]{2,1,0:T(8,128)(2,1)S(1)} async-done(((bf16[32,32,512]{2,1,0:T(8,128)(2,1)}), bf16[32,32,512]{2,1,0:T(8,128)(2,1)S(1)}, u32[]{:S(2)}, u32[]{:S(2)}) %all-to-all-start.1) | async-done | bytes 1048608 | tf_op jit(solution)/shard_map/all_to_all | solution.py:87
  104.9 0.7 convolution_convert_fusion.2
  105.5 0.8 copy.22
  (1 shorter events, 0.0 us)
Async XLA Ops:
  0.6 65.3 %copy-start = (bf16[1,1,2,512,512]{4,3,2,1,0:T(8,128)(2,1)S(1)}, bf16[1,1,2,512,512]{4,3,2,1,0:T(8,128)(2,1)}, u32[]{:S(2)}) copy-start(bf16[1,1,2,512,512]{4,3,2,1,0:T(8,128)(2,1)} %param.11) | copy-start | bytes 3145732
  0.6 5.3 %copy-start.2 = (bf16[1,32,28672]{2,1,0:T(8,128)(2,1)S(1)}, bf16[1,32,28672]{2,1,0:T(8,128)(2,1)}, u32[]{:S(2)}) copy-start(bf16[1,32,28672]{2,1,0:T(8,128)(2,1)} %param.6) | copy-start | bytes 5505028
  2.2 11.6 %copy-start.3 = (s32[2,56]{1,0:T(2,128)S(1)}, s32[2,56]{1,0:T(2,128)}, u32[]{:S(2)}) copy-start(s32[2,56]{1,0:T(2,128)} %param.7) | copy-start | bytes 1348
  3.2 2.8 %collective-permute-start = (bf16[32,14336]{1,0:T(8,128)(2,1)}, bf16[32,14336]{1,0:T(8,128)(2,1)}, u32[]{:S(2)}, u32[]{:S(2)}) collective-permute-start(bf16[32,14336]{1,0:T(8,128)(2,1)} %pad_maximum_fusion), channel_id=1, source_target_pairs={{0,1},{1,0},{2,3},{3,2},{4,5},{5,4},{6,7},{7,6},{8,9},{9,8},{10,11... | collective-permute-start | bytes 2752520 | tf_op jit(solution)/shard_map/ppermute | solution.py:38
  8.0 9.3 %collective-permute-start.1 = (bf16[32,3584]{1,0:T(8,128)(2,1)}, bf16[32,3584]{1,0:T(8,128)(2,1)}, u32[]{:S(2)}, u32[]{:S(2)}) collective-permute-start(bf16[32,3584]{1,0:T(8,128)(2,1)} %get-tuple-element.3), channel_id=1, source_target_pairs={{0,2},{1,3},{2,4},{3,5},{4,6},{5,7},{6,0},{7,1},{8,10},{9,11},{10,... | collective-permute-start | bytes 688136 | tf_op jit(solution)/shard_map/ppermute | solution.py:46
  9.6 13.8 %collective-permute-start.2 = (bf16[32,3584]{1,0:T(8,128)(2,1)S(1)}, bf16[32,3584]{1,0:T(8,128)(2,1)}, u32[]{:S(2)}, u32[]{:S(2)}) collective-permute-start(bf16[32,3584]{1,0:T(8,128)(2,1)S(1)} %get-tuple-element.5), channel_id=1, source_target_pairs={{0,4},{1,5},{2,6},{3,7},{4,0},{5,1},{6,2},{7,3},{8,12},{9,13},{10,... | collective-permute-start | bytes 688136 | tf_op jit(solution)/shard_map/ppermute | solution.py:46
  12.5 10.9 %collective-permute-start.3 = (bf16[32,3584]{1,0:T(8,128)(2,1)S(1)}, bf16[32,3584]{1,0:T(8,128)(2,1)}, u32[]{:S(2)}, u32[]{:S(2)}) collective-permute-start(bf16[32,3584]{1,0:T(8,128)(2,1)S(1)} %get-tuple-element.4), channel_id=1, source_target_pairs={{0,6},{1,7},{2,0},{3,1},{4,2},{5,3},{6,4},{7,5},{8,14},{9,15},{10,... | collective-permute-start | bytes 688136 | tf_op jit(solution)/shard_map/ppermute | solution.py:46
  26.2 39.8 %copy-start.4 = (bf16[1,1,2,512,512]{4,3,2,1,0:T(8,128)(2,1)S(1)}, bf16[1,1,2,512,512]{4,3,2,1,0:T(8,128)(2,1)}, u32[]{:S(2)}) copy-start(bf16[1,1,2,512,512]{4,3,2,1,0:T(8,128)(2,1)} %param.10) | copy-start | bytes 3145732
  71.6 33.2 %all-to-all-start.1 = ((bf16[32,32,512]{2,1,0:T(8,128)(2,1)}), bf16[32,32,512]{2,1,0:T(8,128)(2,1)S(1)}, u32[]{:S(2)}, u32[]{:S(2)}) async-start(bf16[32,32,512]{2,1,0:T(8,128)(2,1)} %bitcast.13), calls=%async_computation.1 | async-start | bytes 2097152 | tf_op jit(solution)/shard_map/all_to_all | solution.py:87
  76.8 3.9 %copy-start.1 = (f32[1,1,2,512,512]{4,3,2,1,0:T(8,128)S(1)}, f32[1,1,2,512,512]{4,3,2,1,0:T(8,128)}, u32[]{:S(2)}) copy-start(f32[1,1,2,512,512]{4,3,2,1,0:T(8,128)} %param.8) | copy-start | bytes 6291460

commit v2 on v0

v2 whole, which is shorter than its diff:
```python
import functools

import jax
import jax.numpy as jnp
from jax import lax
from jax.experimental import pallas as pl
from jax.experimental.pallas import tpu as pltpu
from jax.sharding import PartitionSpec as P

BETA = 0.9
EPS = 1e-06
VMEM_LIMIT = 24 * 1024 * 1024
ANY = pl.BlockSpec(memory_space=pl.ANY)
VMEM = pl.BlockSpec(memory_space=pltpu.VMEM)
SMEM = pl.BlockSpec(memory_space=pltpu.SMEM)


def params(**kw):
    return pltpu.CompilerParams(vmem_limit_bytes=VMEM_LIMIT, **kw)


def pack_kernel(ring, width, place, shard, sent, sems):
    core = place[1]
    copies = []
    for i in range(ring):
        start = pl.multiple_of((2 * i + 1 - core) * width, width)
        copies.append(
            pltpu.make_async_copy(shard.at[:, pl.ds(start, width)], sent.at[i], sems.at[i])
        )
    for copy in copies:
        copy.start()
    for copy in copies:
        copy.wait()


def pack(shard, place, ring, width):
    return pl.pallas_call(
        functools.partial(pack_kernel, ring, width),
        out_shape=jax.ShapeDtypeStruct((ring, shard.shape[0], width), shard.dtype),
        in_specs=[SMEM, ANY],
        out_specs=ANY,
        scratch_shapes=[pltpu.SemaphoreType.DMA((ring,))],
        compiler_params=params(),
        name="pack",
    )(place, shard)


def pair_kernel(ring, width, place, shard, other, *rest):
    outs, (mine, theirs, sems) = rest[:ring], rest[ring:]
    y_index, core = place[0], place[1]
    copies = []
    for step in range(ring):
        target = lax.rem(y_index + step, ring)
        start = pl.multiple_of((2 * target + core) * width, width)
        copies.append(
            (
                pltpu.make_async_copy(
                    shard.at[:, pl.ds(start, width)], mine.at[step], sems.at[0, step]
                ),
                pltpu.make_async_copy(other.at[target], theirs.at[step], sems.at[1, step]),
            )
        )
    order = list(range(1, ring)) + [0]
    for step in order:
        for copy in copies[step]:
            copy.start()
    for step in order:
        for copy in copies[step]:
            copy.wait()
        total = mine[step].astype(jnp.float32) + theirs[step].astype(jnp.float32)
        outs[step][...] = total.astype(outs[step].dtype)


def pair_sum(shard, other, place, ring, width):
    strip = shard.shape[0]
    shapes = [
        jax.ShapeDtypeStruct((strip, width), jnp.bfloat16 if step else jnp.float32)
        for step in range(ring)
    ]
    return pl.pallas_call(
        functools.partial(pair_kernel, ring, width),
        out_shape=shapes,
        in_specs=[SMEM, ANY, ANY],
        out_specs=[VMEM] * ring,
        scratch_shapes=[
            pltpu.VMEM((ring, strip, width), jnp.bfloat16),
            pltpu.VMEM((ring, strip, width), jnp.bfloat16),
            pltpu.SemaphoreType.DMA((2, ring)),
        ],
        compiler_params=params(),
        name="pair_sum",
    )(place, shard, other)


def slots_kernel(pieces, block, owners, *refs):
    out = refs[-1]
    out[...] = jnp.zeros_like(out)
    for c in range(pieces):
        columns = slice(c * block, (c + 1) * block)
        total = refs[0][:, columns]
        for part in refs[1:-1]:
            total = total + part[:, columns].astype(jnp.float32)
        out[owners[c]] = total.astype(jnp.bfloat16)


def fill_slots(parts, owners, n_fsdp, block):
    strip, width = parts[0].shape
    return pl.pallas_call(
        functools.partial(slots_kernel, width // block, block),
        out_shape=jax.ShapeDtypeStruct((n_fsdp, strip, block), jnp.bfloat16),
        in_specs=[SMEM] + [VMEM] * len(parts),
        out_specs=VMEM,
        compiler_params=params(),
        name="fill_slots",
    )(owners, *parts)


def precondition_kernel(block, g_ref, l_ref, r_ref, out_ref):
    g = g_ref[...].reshape(block, block)
    half = jnp.dot(l_ref[0], g, preferred_element_type=jnp.float32).astype(jnp.bfloat16)
    pre = jnp.dot(half, r_ref[0], preferred_element_type=jnp.float32)
    gfull = g.astype(jnp.float32)
    scale = jnp.sqrt(jnp.mean(gfull * gfull)) / jnp.sqrt(jnp.mean(pre * pre) + EPS)
    out_ref[...] = (scale * pre).astype(jnp.bfloat16).reshape(out_ref.shape)


def precondition(incoming, lroots, rroots):
    n, strip, block = incoming.shape
    slots = lroots.shape[0]
    rows = pl.BlockSpec((n // slots, strip, block), lambda s: (s, 0, 0))
    root = pl.BlockSpec((1, block, block), lambda s: (s, 0, 0))
    return pl.pallas_call(
        functools.partial(precondition_kernel, block),
        out_shape=jax.ShapeDtypeStruct(incoming.shape, jnp.bfloat16),
        grid=(slots,),
        in_specs=[rows, root, root],
        out_specs=rows,
        compiler_params=params(),
        cost_estimate=pl.CostEstimate(
            flops=4 * slots * block**3, bytes_accessed=8 * slots * block**2, transcendentals=0
        ),
        name="precondition",
    )(incoming, lroots, rroots)


def collect_kernel(pieces, block, owners, returned, update, sems):
    copies = [
        pltpu.make_async_copy(
            returned.at[owners[c]], update.at[:, pl.ds(c * block, block)], sems.at[c]
        )
        for c in range(pieces)
    ]
    for copy in copies:
        copy.start()
    for copy in copies:
        copy.wait()


def collect(returned, owners, pieces):
    n, strip, block = returned.shape
    return pl.pallas_call(
        functools.partial(collect_kernel, pieces, block),
        out_shape=jax.ShapeDtypeStruct((strip, pieces * block), returned.dtype),
        in_specs=[SMEM, ANY],
        out_specs=ANY,
        scratch_shapes=[pltpu.SemaphoreType.DMA((pieces,))],
        compiler_params=params(),
        name="collect",
    )(owners, returned)


def statistics(g, left, right):
    block = g.shape[0]
    gram_left = (
        lax.dot_general(g, g, (((1,), (1,)), ((), ())), preferred_element_type=jnp.float32) / block
    )
    gram_right = (
        lax.dot_general(g, g, (((0,), (0,)), ((), ())), preferred_element_type=jnp.float32) / block
    )
    return BETA * left + gram_left, BETA * right + gram_right


def on_device(grads, owner, left_stats, right_stats, left_root, right_root):
    strip = grads.shape[1]
    n_fsdp = lax.axis_size("fsdp")
    n_rep = lax.axis_size("rep")
    block = left_stats.shape[-1]
    slots = left_stats.shape[2]
    width = grads.shape[2] // n_rep
    pieces = width // block
    ring = n_rep // 2
    rep_index = lax.axis_index("rep")
    fsdp_index = lax.axis_index("fsdp")
    place = jnp.stack([rep_index // 2, rep_index % 2]).astype(jnp.int32)
    owners = lax.dynamic_slice(
        owner, (fsdp_index * strip // block, rep_index * pieces), (1, pieces)
    )[0]

    shard = grads[0]
    sent = pack(shard, place, ring, width)
    other = lax.ppermute(sent, "rep", [(i, i + 1 - 2 * (i % 2)) for i in range(n_rep)])
    parts = pair_sum(shard, other, place, ring, width)
    arrived = [
        lax.ppermute(parts[step], "rep", [(i, (i + 2 * step) % n_rep) for i in range(n_rep)])
        for step in range(1, ring)
    ]
    outgoing = fill_slots([parts[0], *arrived], owners, n_fsdp, block)
    incoming = lax.all_to_all(outgoing, "fsdp", split_axis=0, concat_axis=0, tiled=True)
    results = precondition(incoming, left_root[0, 0], right_root[0, 0])
    returned = lax.all_to_all(results, "fsdp", split_axis=0, concat_axis=0, tiled=True)
    new_l, new_r = jax.vmap(statistics)(
        incoming.reshape(slots, block, block), left_stats[0, 0], right_stats[0, 0]
    )
    update = collect(returned, owners, pieces)
    return (update, new_l[None, None], new_r[None, None])


def solution(mesh):
    in_specs = (
        P("rep", "fsdp", None),
        P(),
        P("rep", "fsdp", None, None, None),
        P("rep", "fsdp", None, None, None),
        P("rep", "fsdp", None, None, None),
        P("rep", "fsdp", None, None, None),
    )
    out_specs = (
        P("fsdp", "rep"),
        P("rep", "fsdp", None, None, None),
        P("rep", "fsdp", None, None, None),
    )
    return jax.shard_map(
        on_device, mesh=mesh, in_specs=in_specs, out_specs=out_specs, check_vma=False
    )
```

time: 172 us -> 101 us (0.59)
  the two profiles are of different devices: /device:TPU:24 before, /device:TPU:32 now
where the time goes in v2:
time: 101 us; the launch traced here: 100 us
  blocking collectives  39 us (39%)
  waiting for transfers between devices  33.6 us (33%)
  starting transfers between devices  11.2 us (11%)
  Pallas kernels  8.35 us (8%)
  matrix products  5.97 us (6%)
  local copies, waits for them, and re-layouts  1.6 us (2%)
    all_to_all x1, blocking collectives, on_device(): lax.all_to_all(outgoing, 'fsdp', split_axis=0, concat_axis=0, tiled=True)  39 us
    all_to_all x1, waiting for transfers between devices, on_device(): lax.all_to_all(results, 'fsdp', split_axis=0, concat_axis=0, tiled=True)  22 us
    ppermute x3, waiting for transfers between devices, on_device(): lax.ppermute(parts[step], 'rep', [(i, (i + 2 * step) % n_rep) for i in ra...  9.11 us
    ppermute x3, starting transfers between devices, on_device(): lax.ppermute(parts[step], 'rep', [(i, (i + 2 * step) % n_rep) for i in ra...  5.9 us
    all_to_all x1, starting transfers between devices, on_device(): lax.all_to_all(results, 'fsdp', split_axis=0, concat_axis=0, tiled=True)  5.19 us
    dot_general x1, matrix products, statistics(): lax.dot_general(g, g, (((0,), (0,)), ((), ())), preferred_element_type=jn...  3.9 us
    pallas_call x1, Pallas kernels, precondition(): pl.pallas_call(functools.partial(precondition_kernel, block), out_shape=j...  3.16 us
    ppermute x1, waiting for transfers between devices, on_device(): lax.ppermute(sent, 'rep', [(i, i + 1 - 2 * (i % 2)) for i in range(n_rep)])  2.46 us
  transfers between devices with their start and end apart: 5, of which 4 were waited for; matrix products, arithmetic and copies ran while one was open for 6% of the time, Pallas kernels for 0%

profile of v2, /device:TPU:32, one launch (start us, length us, event | category | flops | bytes accessed | tf_op | source)
XLA Modules:
  0.0 100.5 jit_solution(11785156379700138030)
XLA Ops:
  0.6 0.0 copy-start
  0.7 0.1 pad_add_fusion.place
  0.7 0.0 copy-start.1
  0.7 1.5 %copy-done.1 = bf16[1,32,28672]{2,1,0:T(8,128)(2,1)S(1)} copy-done((bf16[1,32,28672]{2,1,0:T(8,128)(2,1)S(1)}, bf16[1,32,28672]{2,1,0:T(8,128)(2,1)}, u32[]{:S(2)}) %copy-start.1) | copy-done | bytes 1835032
  2.2 0.9 pack.1
  3.1 0.1 collective-permute-start
  3.2 2.5 %collective-permute-done.other = bf16[4,32,3584]{2,1,0:T(8,128)(2,1)S(1)} collective-permute-done((bf16[4,32,3584]{2,1,0:T(8,128)(2,1)S(1)}, bf16[4,32,3584]{2,1,0:T(8,128)(2,1)S(1)}, u32[]{:S(2)}, u32[]{:S(2)}) %collective-permute-start) | collective-permute-done | bytes 917536 | tf_op jit(solution)/shard_map/ppermute | solution.py:201
  5.7 2.3 %pair_sum.1 = (f32[32,3584]{1,0:T(8,128)S(1)}, bf16[32,3584]{1,0:T(8,128)(2,1)S(1)}, bf16[32,3584]{1,0:T(8,128)(2,1)S(1)}, bf16[32,3584]{1,0:T(8,128)(2,1)S(1)}) custom-call(s32[2]{0:T(128)S(1)} %pad_add_fusion.place, bf16[32,28672]{1,0:T(8,128)(2,1)S(1)} %bitcast.27, bf16[4,32,3584]{2,1,0:T(8,128)(2,1)S(1)} %collective-permute-done.other), custom_call_target="tpu_custom_call" | custom-call | tf_op jit(solution)/shard_map/pair_sum/pallas_call | solution.py:80
  8.0 1.7 %collective-permute-start.1 = (bf16[32,3584]{1,0:T(8,128)(2,1)S(1)}, bf16[32,3584]{1,0:T(8,128)(2,1)S(1)}, u32[]{:S(2)}, u32[]{:S(2)}) collective-permute-start(bf16[32,3584]{1,0:T(8,128)(2,1)S(1)} %get-tuple-element.8), channel_id=1, source_target_pairs={{0,2},{1,3},{2,4},{3,5},{4,6},{5,7},{6,0},{7,1},{8,10},{9,11},{10,... | collective-permute-start | bytes 688136 | tf_op jit(solution)/shard_map/ppermute | solution.py:204
  9.7 2.9 %collective-permute-start.2 = (bf16[32,3584]{1,0:T(8,128)(2,1)S(1)}, bf16[32,3584]{1,0:T(8,128)(2,1)S(1)}, u32[]{:S(2)}, u32[]{:S(2)}) collective-permute-start(bf16[32,3584]{1,0:T(8,128)(2,1)S(1)} %get-tuple-element.9), channel_id=1, source_target_pairs={{0,4},{1,5},{2,6},{3,7},{4,0},{5,1},{6,2},{7,3},{8,12},{9,13},{10,... | collective-permute-start | bytes 688136 | tf_op jit(solution)/shard_map/ppermute | solution.py:204
  12.6 1.3 %collective-permute-start.3 = (bf16[32,3584]{1,0:T(8,128)(2,1)S(1)}, bf16[32,3584]{1,0:T(8,128)(2,1)S(1)}, u32[]{:S(2)}, u32[]{:S(2)}) collective-permute-start(bf16[32,3584]{1,0:T(8,128)(2,1)S(1)} %get-tuple-element.10), channel_id=1, source_target_pairs={{0,6},{1,7},{2,0},{3,1},{4,2},{5,3},{6,4},{7,5},{8,14},{9,15},{10,... | collective-permute-start | bytes 688136 | tf_op jit(solution)/shard_map/ppermute | solution.py:204
  13.9 0.0 copy-done
  13.9 0.1 dynamic-slice_bitcast_fusion.owners
  14.0 3.0 %collective-permute-done.1.refs_1_ = bf16[32,3584]{1,0:T(8,128)(2,1)S(1)} collective-permute-done((bf16[32,3584]{1,0:T(8,128)(2,1)S(1)}, bf16[32,3584]{1,0:T(8,128)(2,1)S(1)}, u32[]{:S(2)}, u32[]{:S(2)}) %collective-permute-start.1) | collective-permute-done | bytes 229408 | tf_op jit(solution)/shard_map/ppermute | solution.py:204
  17.0 6.1 %collective-permute-done.2.refs_2_ = bf16[32,3584]{1,0:T(8,128)(2,1)S(1)} collective-permute-done((bf16[32,3584]{1,0:T(8,128)(2,1)S(1)}, bf16[32,3584]{1,0:T(8,128)(2,1)S(1)}, u32[]{:S(2)}, u32[]{:S(2)}) %collective-permute-start.2) | collective-permute-done | bytes 229408 | tf_op jit(solution)/shard_map/ppermute | solution.py:204
  23.1 0.0 collective-permute-done.3.refs_3_
  23.1 0.0 copy-start.2
  23.1 0.0 copy-start.3
  23.1 0.7 fill_slots.1
  23.8 39.0 %all_to_all.10.g_ref = bf16[32,32,512]{2,1,0:T(8,128)(2,1)S(1)} all-to-all(bf16[32,32,512]{2,1,0:T(8,128)(2,1)S(1)} %fill_slots.1), channel_id=1, replica_groups=mesh['fsdp'=32,'rep'=8] {'fsdp'}, dimensions={0} | all-to-all | bytes 2097152 | tf_op jit(solution)/shard_map/all_to_all | solution.py:208
  62.8 0.0 copy-done.2
  62.8 0.0 copy-done.3
  62.8 3.2 %precondition.1 = bf16[32,32,512]{2,1,0:T(8,128)(2,1)} custom-call(bf16[32,32,512]{2,1,0:T(8,128)(2,1)S(1)} %all_to_all.10.g_ref, bf16[2,512,512]{2,1,0:T(8,128)(2,1)S(1)} %bitcast.28, bf16[2,512,512]{2,1,0:T(8,128)(2,1)S(1)} %bitcast.29), custom_call_target="tpu_custom_call" | custom-call | flops 1073741824 | bytes 4194304 | tf_op jit(solution)/shard_map/precondition/pallas_call | solution.py:132
  66.0 5.2 %all-to-all-start.1 = ((bf16[32,32,512]{2,1,0:T(8,128)(2,1)}), bf16[32,32,512]{2,1,0:T(8,128)(2,1)S(1)}, u32[]{:S(2)}, u32[]{:S(2)}) async-start(bf16[32,32,512]{2,1,0:T(8,128)(2,1)} %precondition.1), calls=%async_computation.1 | async-start | bytes 2097152 | tf_op jit(solution)/shard_map/all_to_all | solution.py:210
  71.2 0.0 copy-start.4
  71.2 3.9 %fusion = f32[1,1,2,512,512]{4,3,2,1,0:T(8,128)} fusion(f32[1,1,2,512,512]{4,3,2,1,0:T(8,128)} %param.9, bf16[2,512,512]{2,1,0:T(8,128)(2,1)S(1)} %bitcast.24), kind=kOutput, calls=%fused_computation.1 | convolution fusion | flops 538443776 | bytes 5242880 | tf_op jit(solution)/shard_map/vmap()/dot_general | solution.py:178
  75.1 0.0 copy-done.4
  75.1 2.1 %fusion.1 = f32[1,1,2,512,512]{4,3,2,1,0:T(8,128)} fusion(f32[1,1,2,512,512]{4,3,2,1,0:T(8,128)S(1)} %copy-done.4, bf16[2,512,512]{2,1,0:T(8,128)(2,1)S(1)} %bitcast.25), kind=kOutput, calls=%fused_computation.3 | convolution fusion | flops 538443776 | bytes 5242880 | tf_op jit(solution)/shard_map/vmap()/dot_general | solution.py:175
  77.2 22.0 %all-to-all-done.1.returned = bf16[32,32,512]{2,1,0:T(8,128)(2,1)S(1)} async-done(((bf16[32,32,512]{2,1,0:T(8,128)(2,1)}), bf16[32,32,512]{2,1,0:T(8,128)(2,1)S(1)}, u32[]{:S(2)}, u32[]{:S(2)}) %all-to-all-start.1) | async-done | bytes 1048608 | tf_op jit(solution)/shard_map/all_to_all | solution.py:210
  99.2 1.3 %collect.1 = bf16[32,3584]{1,0:T(8,128)(2,1)} custom-call(s32[7]{0:T(128)S(1)} %dynamic-slice_bitcast_fusion.owners, bf16[32,32,512]{2,1,0:T(8,128)(2,1)S(1)} %all-to-all-done.1.returned), custom_call_target="tpu_custom_call" | custom-call | tf_op jit(solution)/shard_map/collect/pallas_call | solution.py:161
Async XLA Ops:
  0.6 13.3 %copy-start = (s32[2,56]{1,0:T(2,128)S(1)}, s32[2,56]{1,0:T(2,128)}, u32[]{:S(2)}) copy-start(s32[2,56]{1,0:T(2,128)} %param.7) | copy-start | bytes 1348
  0.7 1.5 %copy-start.1 = (bf16[1,32,28672]{2,1,0:T(8,128)(2,1)S(1)}, bf16[1,32,28672]{2,1,0:T(8,128)(2,1)}, u32[]{:S(2)}) copy-start(bf16[1,32,28672]{2,1,0:T(8,128)(2,1)} %param.6) | copy-start | bytes 5505028
  3.1 2.6 %collective-permute-start = (bf16[4,32,3584]{2,1,0:T(8,128)(2,1)S(1)}, bf16[4,32,3584]{2,1,0:T(8,128)(2,1)S(1)}, u32[]{:S(2)}, u32[]{:S(2)}) collective-permute-start(bf16[4,32,3584]{2,1,0:T(8,128)(2,1)S(1)} %pack.1), channel_id=1, source_target_pairs={{0,1},{1,0},{2,3},{3,2},{4,5},{5,4},{6,7},{7,6},{8,9},{9,8},{10,11... | collective-permute-start | bytes 2752520 | tf_op jit(solution)/shard_map/ppermute | solution.py:201
  8.0 9.0 %collective-permute-start.1 = (bf16[32,3584]{1,0:T(8,128)(2,1)S(1)}, bf16[32,3584]{1,0:T(8,128)(2,1)S(1)}, u32[]{:S(2)}, u32[]{:S(2)}) collective-permute-start(bf16[32,3584]{1,0:T(8,128)(2,1)S(1)} %get-tuple-element.8), channel_id=1, source_target_pairs={{0,2},{1,3},{2,4},{3,5},{4,6},{5,7},{6,0},{7,1},{8,10},{9,11},{10,... | collective-permute-start | bytes 688136 | tf_op jit(solution)/shard_map/ppermute | solution.py:204
  9.7 13.4 %collective-permute-start.2 = (bf16[32,3584]{1,0:T(8,128)(2,1)S(1)}, bf16[32,3584]{1,0:T(8,128)(2,1)S(1)}, u32[]{:S(2)}, u32[]{:S(2)}) collective-permute-start(bf16[32,3584]{1,0:T(8,128)(2,1)S(1)} %get-tuple-element.9), channel_id=1, source_target_pairs={{0,4},{1,5},{2,6},{3,7},{4,0},{5,1},{6,2},{7,3},{8,12},{9,13},{10,... | collective-permute-start | bytes 688136 | tf_op jit(solution)/shard_map/ppermute | solution.py:204
  12.6 10.5 %collective-permute-start.3 = (bf16[32,3584]{1,0:T(8,128)(2,1)S(1)}, bf16[32,3584]{1,0:T(8,128)(2,1)S(1)}, u32[]{:S(2)}, u32[]{:S(2)}) collective-permute-start(bf16[32,3584]{1,0:T(8,128)(2,1)S(1)} %get-tuple-element.10), channel_id=1, source_target_pairs={{0,6},{1,7},{2,0},{3,1},{4,2},{5,3},{6,4},{7,5},{8,14},{9,15},{10,... | collective-permute-start | bytes 688136 | tf_op jit(solution)/shard_map/ppermute | solution.py:204
  23.1 39.7 %copy-start.2 = (bf16[1,1,2,512,512]{4,3,2,1,0:T(8,128)(2,1)S(1)}, bf16[1,1,2,512,512]{4,3,2,1,0:T(8,128)(2,1)}, u32[]{:S(2)}) copy-start(bf16[1,1,2,512,512]{4,3,2,1,0:T(8,128)(2,1)} %param.10) | copy-start | bytes 3145732
  23.1 39.7 %copy-start.3 = (bf16[1,1,2,512,512]{4,3,2,1,0:T(8,128)(2,1)S(1)}, bf16[1,1,2,512,512]{4,3,2,1,0:T(8,128)(2,1)}, u32[]{:S(2)}) copy-start(bf16[1,1,2,512,512]{4,3,2,1,0:T(8,128)(2,1)} %param.11) | copy-start | bytes 3145732
  66.0 33.2 %all-to-all-start.1 = ((bf16[32,32,512]{2,1,0:T(8,128)(2,1)}), bf16[32,32,512]{2,1,0:T(8,128)(2,1)S(1)}, u32[]{:S(2)}, u32[]{:S(2)}) async-start(bf16[32,32,512]{2,1,0:T(8,128)(2,1)} %precondition.1), calls=%async_computation.1 | async-start | bytes 2097152 | tf_op jit(solution)/shard_map/all_to_all | solution.py:210
  71.2 3.9 %copy-start.4 = (f32[1,1,2,512,512]{4,3,2,1,0:T(8,128)S(1)}, f32[1,1,2,512,512]{4,3,2,1,0:T(8,128)}, u32[]{:S(2)}) copy-start(f32[1,1,2,512,512]{4,3,2,1,0:T(8,128)} %param.8) | copy-start | bytes 6291460

commit v3 on v2

v3 whole, which is shorter than its diff:
```python
import functools

import jax
import jax.numpy as jnp
from jax import lax
from jax.experimental import pallas as pl
from jax.experimental.pallas import tpu as pltpu
from jax.sharding import PartitionSpec as P

BETA = 0.9
EPS = 1e-06
TOKEN = (16, 128)
Y_ORDER = (2, 1, 3)
VMEM_LIMIT = 24 * 1024 * 1024
ANY = pl.BlockSpec(memory_space=pl.ANY)
HBM = pl.BlockSpec(memory_space=pltpu.HBM)
VMEM = pl.BlockSpec(memory_space=pltpu.VMEM)
CHEAP = pl.CostEstimate(flops=1, bytes_accessed=1, transcendentals=0)
COPY = pl.CostEstimate(flops=1, bytes_accessed=2**21, transcendentals=0)
SMEM = pl.BlockSpec(memory_space=pltpu.SMEM)


def params(**kw):
    return pltpu.CompilerParams(vmem_limit_bytes=VMEM_LIMIT, **kw)


def groups_kernel(ring, width, other, shard, *refs):
    out, sems = refs[-2:]
    rep_index = lax.axis_index("rep")
    core = lax.rem(rep_index, 2)
    if other:
        core = 1 - core
    copies = []
    for step in range(ring):
        target = lax.rem(rep_index // 2 + step, ring)
        start = pl.multiple_of((2 * target + core) * width, width)
        copies.append(
            pltpu.make_async_copy(shard.at[:, pl.ds(start, width)], out.at[step], sems.at[step])
        )
    for copy in copies:
        copy.start()
    for copy in copies:
        copy.wait()


def groups(shard, ring, width, other, *after):
    return pl.pallas_call(
        functools.partial(groups_kernel, ring, width, other),
        out_shape=jax.ShapeDtypeStruct((ring, shard.shape[0], width), shard.dtype),
        in_specs=[HBM] + [ANY] * len(after),
        out_specs=VMEM,
        scratch_shapes=[pltpu.SemaphoreType.DMA((ring,))],
        compiler_params=params(),
        cost_estimate=COPY,
        name="groups",
    )(pltpu.with_memory_space_constraint(shard, pltpu.HBM), *after)


def pair_kernel(ring, kept, other, *refs):
    outs = refs[-ring:]
    for step in range(ring):
        outs[step][...] = kept[step] + other[step]


def pair_sum(kept, other, *after):
    ring = kept.shape[0]
    return pl.pallas_call(
        functools.partial(pair_kernel, ring),
        out_shape=[jax.ShapeDtypeStruct(kept.shape[1:], kept.dtype)] * ring,
        in_specs=[VMEM, VMEM] + [ANY] * len(after),
        out_specs=[VMEM] * ring,
        compiler_params=params(),
        cost_estimate=CHEAP,
        name="pair_sum",
    )(kept, other, *after)


def total_of(parts, columns):
    total = parts[0][:, columns].astype(jnp.float32)
    for part in parts[1:]:
        total = total + part[:, columns].astype(jnp.float32)
    return total.astype(jnp.bfloat16)


def total_kernel(block, *refs):
    out, token = refs[-2:]
    for c in range(out.shape[1] // block):
        columns = slice(c * block, (c + 1) * block)
        out[:, columns] = total_of(refs[:-2], columns)
    token[...] = jnp.zeros_like(token)


def add_up(parts, block):
    return pl.pallas_call(
        functools.partial(total_kernel, block),
        out_shape=[
            jax.ShapeDtypeStruct(parts[0].shape, jnp.bfloat16),
            jax.ShapeDtypeStruct(TOKEN, jnp.bfloat16),
        ],
        in_specs=[VMEM] * len(parts),
        out_specs=[VMEM] * 2,
        compiler_params=params(),
        cost_estimate=CHEAP,
        name="add_up",
    )(*parts)


def slots_kernel(pieces, block, n_parts, owners, *refs):
    parts, out = refs[:n_parts], refs[-1]
    out[...] = jnp.zeros_like(out)
    for c in range(pieces):
        out[owners[c]] = total_of(parts, slice(c * block, (c + 1) * block))


def fill_slots(parts, owners, n_fsdp, block, *after):
    strip, width = parts[0].shape
    return pl.pallas_call(
        functools.partial(slots_kernel, width // block, block, len(parts)),
        out_shape=jax.ShapeDtypeStruct((n_fsdp, strip, block), jnp.bfloat16),
        in_specs=[SMEM] + [VMEM] * len(parts) + [ANY] * len(after),
        out_specs=VMEM,
        compiler_params=params(),
        cost_estimate=CHEAP,
        name="fill_slots",
    )(owners, *parts, *after)


def precondition_kernel(g_ref, l_ref, r_ref, out_ref):
    slots, block, _ = l_ref.shape
    rows = g_ref.shape[0] // slots
    for b in range(slots):
        g = g_ref[b * rows : (b + 1) * rows].reshape(block, block)
        half = jnp.dot(l_ref[b], g, preferred_element_type=jnp.float32).astype(jnp.bfloat16)
        pre = jnp.dot(half, r_ref[b], preferred_element_type=jnp.float32)
        gfull = g.astype(jnp.float32)
        scale = jnp.sqrt(jnp.mean(gfull * gfull)) / jnp.sqrt(jnp.mean(pre * pre) + EPS)
        out_ref[b * rows : (b + 1) * rows] = (
            (scale * pre).astype(jnp.bfloat16).reshape(rows, *g_ref.shape[1:])
        )


def precondition(incoming, lroots, rroots):
    slots, block, _ = lroots.shape
    return pl.pallas_call(
        precondition_kernel,
        out_shape=jax.ShapeDtypeStruct(incoming.shape, jnp.bfloat16),
        in_specs=[VMEM] * 3,
        out_specs=VMEM,
        compiler_params=params(),
        cost_estimate=pl.CostEstimate(
            flops=4 * slots * block**3, bytes_accessed=8 * slots * block**2, transcendentals=0
        ),
        name="precondition",
    )(incoming, lroots, rroots)


def collect_kernel(pieces, block, owners, returned, update, sems):
    copies = [
        pltpu.make_async_copy(
            returned.at[owners[c]], update.at[:, pl.ds(c * block, block)], sems.at[c]
        )
        for c in range(pieces)
    ]
    for copy in copies:
        copy.start()
    for copy in copies:
        copy.wait()


def collect(returned, owners, pieces):
    n, strip, block = returned.shape
    return pl.pallas_call(
        functools.partial(collect_kernel, pieces, block),
        out_shape=jax.ShapeDtypeStruct((strip, pieces * block), returned.dtype),
        in_specs=[SMEM, ANY],
        out_specs=ANY,
        scratch_shapes=[pltpu.SemaphoreType.DMA((pieces,))],
        compiler_params=params(),
        name="collect",
    )(owners, returned)


def statistics(g, left, right):
    block = g.shape[0]
    gram_left = (
        lax.dot_general(g, g, (((1,), (1,)), ((), ())), preferred_element_type=jnp.float32) / block
    )
    gram_right = (
        lax.dot_general(g, g, (((0,), (0,)), ((), ())), preferred_element_type=jnp.float32) / block
    )
    return BETA * left + gram_left, BETA * right + gram_right


def on_device(grads, owner, left_stats, right_stats, left_root, right_root):
    strip = grads.shape[1]
    n_fsdp = lax.axis_size("fsdp")
    n_rep = lax.axis_size("rep")
    block = left_stats.shape[-1]
    slots = left_stats.shape[2]
    width = grads.shape[2] // n_rep
    pieces = width // block
    ring = n_rep // 2
    rep_index = lax.axis_index("rep")
    fsdp_index = lax.axis_index("fsdp")
    owners = lax.dynamic_slice(
        owner, (fsdp_index * strip // block, rep_index * pieces), (1, pieces)
    )[0]

    core = rep_index % 2
    swap = [(i, i + 1 - 2 * (i % 2)) for i in range(n_rep)]
    other = lax.ppermute(groups(grads[0], ring, width, True), "rep", swap)
    parts = pair_sum(groups(grads[0], ring, width, False), other)

    def along_y(parts):
        arrived = [
            lax.ppermute(parts[step], "rep", [(i, (i + 2 * step) % n_rep) for i in range(n_rep)])
            for step in Y_ORDER
        ]
        return [parts[0], *arrived]

    total, token = lax.cond(
        core == 0,
        lambda parts: tuple(add_up(along_y(parts), block)),
        lambda parts: (parts[0], jnp.zeros(TOKEN, jnp.bfloat16)),
        parts,
    )
    token = lax.ppermute(token, "rep", swap)
    outgoing = lax.cond(
        core == 1,
        lambda parts, total, token, owners: fill_slots(
            along_y(parts), owners, n_fsdp, block, token
        ),
        lambda parts, total, token, owners: fill_slots([total], owners, n_fsdp, block),
        parts, total, token, owners,
    )
    incoming = lax.all_to_all(outgoing, "fsdp", split_axis=0, concat_axis=0, tiled=True)
    results = precondition(incoming, left_root[0, 0], right_root[0, 0])
    returned = lax.all_to_all(results, "fsdp", split_axis=0, concat_axis=0, tiled=True)
    new_l, new_r = jax.vmap(statistics)(
        incoming.reshape(slots, block, block), left_stats[0, 0], right_stats[0, 0]
    )
    update = collect(returned, owners, pieces)
    return (update, new_l[None, None], new_r[None, None])


def solution(mesh):
    in_specs = (
        P("rep", "fsdp", None),
        P(),
        P("rep", "fsdp", None, None, None),
        P("rep", "fsdp", None, None, None),
        P("rep", "fsdp", None, None, None),
        P("rep", "fsdp", None, None, None),
    )
    out_specs = (
        P("fsdp", "rep"),
        P("rep", "fsdp", None, None, None),
        P("rep", "fsdp", None, None, None),
    )
    return jax.shard_map(
        on_device, mesh=mesh, in_specs=in_specs, out_specs=out_specs, check_vma=False
    )
```

time: 101 us -> 92.6 us (0.917)
  the two profiles are of different devices: /device:TPU:32 before, /device:TPU:1 now
where the time goes in v3:
time: 92.6 us; the launch traced here: 92.2 us
  blocking collectives  30.1 us (33%)
  starting transfers between devices  23.1 us (25%)
  waiting for transfers between devices  22.9 us (25%)
  Pallas kernels  9.29 us (10%)
  matrix products  5.97 us (6%)
    all_to_all x1, blocking collectives, on_device(): lax.all_to_all(outgoing, 'fsdp', split_axis=0, concat_axis=0, tiled=True)  30.1 us
    all_to_all x1, waiting for transfers between devices, on_device(): lax.all_to_all(results, 'fsdp', split_axis=0, concat_axis=0, tiled=True)  16.2 us
    ppermute x1, starting transfers between devices, on_device(): token = lax.ppermute(token, 'rep', swap)  10.7 us
    all_to_all x1, starting transfers between devices, on_device(): lax.all_to_all(results, 'fsdp', split_axis=0, concat_axis=0, tiled=True)  5.22 us
    ppermute x3, waiting for transfers between devices, along_y(): lax.ppermute(parts[step], 'rep', [(i, (i + 2 * step) % n_rep) for i in ra...  5.19 us
    dot_general x1, matrix products, statistics(): lax.dot_general(g, g, (((0,), (0,)), ((), ())), preferred_element_type=jn...  3.9 us
    ppermute x3, starting transfers between devices, along_y(): lax.ppermute(parts[step], 'rep', [(i, (i + 2 * step) % n_rep) for i in ra...  3.85 us
    ppermute x1, starting transfers between devices, on_device(): other = lax.ppermute(groups(grads[0], ring, width, True), 'rep', swap)  3.33 us
  transfers between devices with their start and end apart: 6, of which 5 were waited for; matrix products, arithmetic and copies ran while one was open for 7% of the time, Pallas kernels for 1%

profile of v3, /device:TPU:1, one launch (start us, length us, event | category | flops | bytes accessed | tf_op | source)
XLA Modules:
  0.0 92.2 jit_solution(12698863635501874503)
XLA Ops:
  0.6 0.0 copy-start
  0.6 1.3 %groups.3 = bf16[4,32,3584]{2,1,0:T(8,128)(2,1)S(1)} custom-call(bf16[32,28672]{1,0:T(8,128)(2,1)} %bitcast.26), custom_call_target="tpu_custom_call" | custom-call | flops 1 | bytes 2097152 | tf_op jit(solution)/shard_map/groups/pallas_call | solution.py:47
  2.0 3.3 %collective-permute-start.6 = (bf16[4,32,3584]{2,1,0:T(8,128)(2,1)S(1)}, bf16[4,32,3584]{2,1,0:T(8,128)(2,1)S(1)}, u32[]{:S(2)}, u32[]{:S(2)}) collective-permute-start(bf16[4,32,3584]{2,1,0:T(8,128)(2,1)S(1)} %groups.3), channel_id=1, source_target_pairs={{0,1},{1,0},{2,3},{3,2},{4,5},{5,4},{6,7},{7,6},{8,9},{9,8},{10,11... | collective-permute-start | bytes 2752520 | tf_op jit(solution)/shard_map/ppermute | solution.py:211
  5.3 1.3 %groups.2.kept = bf16[4,32,3584]{2,1,0:T(8,128)(2,1)S(1)} custom-call(bf16[32,28672]{1,0:T(8,128)(2,1)} %bitcast.27), custom_call_target="tpu_custom_call" | custom-call | flops 1 | bytes 2097152 | tf_op jit(solution)/shard_map/groups/pallas_call | solution.py:47
  6.7 0.7 collective-permute-done.6.other
  7.4 0.9 pair_sum.1
  8.3 10.7 %collective-permute-start.7 = (bf16[16,128]{1,0:T(8,128)(2,1)S(1)}, bf16[16,128]{1,0:T(8,128)(2,1)S(1)}, u32[]{:S(2)}, u32[]{:S(2)}) collective-permute-start(bf16[16,128]{1,0:T(8,128)(2,1)S(1)} %get-tuple-element.54), channel_id=1, source_target_pairs={{0,1},{1,0},{2,3},{3,2},{4,5},{5,4},{6,7},{7,6},{8,9},{9,8},{10,11... | collective-permute-start | bytes 12296 | tf_op jit(solution)/shard_map/ppermute | solution.py:227
  19.1 0.0 copy-done
  19.1 0.1 dynamic-slice_bitcast_fusion.owners
  19.1 0.7 collective-permute-done.7
  19.9 0.0 copy-start.1
  19.9 0.0 copy-start.2
  19.9 10.7 %conditional.3 = (bf16[32,32,512]{2,1,0:T(8,128)(2,1)}) conditional(s32[]{:T(128)} %convert_element_type.6, (s32[7]{0:T(128)S(1)}, bf16[32,3584]{1,0:T(8,128)(2,1)S(1)}) %tuple.22, (bf16[32,3584]{1,0:T(8,128)(2,1)}, bf16[32,3584]{1,0:T(8,128)(2,1)S(1)}, bf16[32,3584]{1,0:T(8,128)(2,1)}, s32[7]{0:T(128)S(1)}, bf16[32,3584]{1,0:T(8,128)(2,1)S(1)}, ...), branch_computations={%region_2.3_spmd, %region_3.4_spmd} | conditional | flops 1 | bytes 2752641 | solution.py:228
  19.9 1.2 %collective-permute-start.3 = (bf16[32,3584]{1,0:T(8,128)(2,1)}, bf16[32,3584]{1,0:T(8,128)(2,1)S(1)}, u32[]{:S(2)}, u32[]{:S(2)}) collective-permute-start(bf16[32,3584]{1,0:T(8,128)(2,1)} %get-tuple-element.36), channel_id=1, source_target_pairs={{0,4},{1,5},{2,6},{3,7},{4,0},{5,1},{6,2},{7,3},{8,12},{9,13},{10,... | collective-permute-start | bytes 688136 | tf_op jit(solution)/shard_map/cond/branch_1_fun/ppermute | solution.py:216
  21.1 1.1 %collective-permute-start.4 = (bf16[32,3584]{1,0:T(8,128)(2,1)S(1)}, bf16[32,3584]{1,0:T(8,128)(2,1)S(1)}, u32[]{:S(2)}, u32[]{:S(2)}) collective-permute-start(bf16[32,3584]{1,0:T(8,128)(2,1)S(1)} %get-tuple-element.37), channel_id=1, source_target_pairs={{0,2},{1,3},{2,4},{3,5},{4,6},{5,7},{6,0},{7,1},{8,10},{9,11},{10,... | collective-permute-start | bytes 688136 | tf_op jit(solution)/shard_map/cond/branch_1_fun/ppermute | solution.py:216
  22.1 1.6 %collective-permute-start.5 = (bf16[32,3584]{1,0:T(8,128)(2,1)}, bf16[32,3584]{1,0:T(8,128)(2,1)S(1)}, u32[]{:S(2)}, u32[]{:S(2)}) collective-permute-start(bf16[32,3584]{1,0:T(8,128)(2,1)} %get-tuple-element.38), channel_id=1, source_target_pairs={{0,6},{1,7},{2,0},{3,1},{4,2},{5,3},{6,4},{7,5},{8,14},{9,15},{10,... | collective-permute-start | bytes 688136 | tf_op jit(solution)/shard_map/cond/branch_1_fun/ppermute | solution.py:216
  23.7 2.8 %collective-permute-done.3.refs_1_ = bf16[32,3584]{1,0:T(8,128)(2,1)S(1)} collective-permute-done((bf16[32,3584]{1,0:T(8,128)(2,1)}, bf16[32,3584]{1,0:T(8,128)(2,1)S(1)}, u32[]{:S(2)}, u32[]{:S(2)}) %collective-permute-start.3) | collective-permute-done | bytes 229408 | tf_op jit(solution)/shard_map/cond/branch_1_fun/ppermute | solution.py:216
  26.6 2.4 %collective-permute-done.4.refs_2_ = bf16[32,3584]{1,0:T(8,128)(2,1)S(1)} collective-permute-done((bf16[32,3584]{1,0:T(8,128)(2,1)S(1)}, bf16[32,3584]{1,0:T(8,128)(2,1)S(1)}, u32[]{:S(2)}, u32[]{:S(2)}) %collective-permute-start.4) | collective-permute-done | bytes 229408 | tf_op jit(solution)/shard_map/cond/branch_1_fun/ppermute | solution.py:216
  28.9 0.0 collective-permute-done.5.refs_3_
  28.9 1.7 %fill_slots.3 = bf16[32,32,512]{2,1,0:T(8,128)(2,1)} custom-call(s32[7]{0:T(128)S(1)} %get-tuple-element.34.owners, bf16[32,3584]{1,0:T(8,128)(2,1)S(1)} %get-tuple-element.35.refs_0_, bf16[32,3584]{1,0:T(8,128)(2,1)S(1)} %collective-permute-done.3.refs_1_, bf16[32,3584]{1,0:T(8,128)(2,1)S(1)} %collective-permute-done.4.refs_2_, ...), custom_call_target="tpu_custom_call" | custom-call | flops 1 | bytes 1 | tf_op jit(solution)/shard_map/cond/branch_1_fun/fill_slots/pallas_call | solution.py:117
  30.6 30.1 %all_to_all.10.g_ref = bf16[32,32,512]{2,1,0:T(8,128)(2,1)S(1)} all-to-all(bf16[32,32,512]{2,1,0:T(8,128)(2,1)} %get-tuple-element.60), channel_id=1, replica_groups=mesh['fsdp'=32,'rep'=8] {'fsdp'}, dimensions={0} | all-to-all | bytes 2097152 | tf_op jit(solution)/shard_map/all_to_all | solution.py:236
  60.7 0.0 copy-done.1
  60.7 0.0 copy-done.2
  60.7 2.8 %precondition.1 = bf16[32,32,512]{2,1,0:T(8,128)(2,1)} custom-call(bf16[32,32,512]{2,1,0:T(8,128)(2,1)S(1)} %all_to_all.10.g_ref, bf16[2,512,512]{2,1,0:T(8,128)(2,1)S(1)} %bitcast.24, bf16[2,512,512]{2,1,0:T(8,128)(2,1)S(1)} %bitcast.25), custom_call_target="tpu_custom_call" | custom-call | flops 1073741824 | bytes 4194304 | tf_op jit(solution)/shard_map/precondition/pallas_call | solution.py:144
  63.5 5.2 %all-to-all-start.1 = ((bf16[32,32,512]{2,1,0:T(8,128)(2,1)}), bf16[32,32,512]{2,1,0:T(8,128)(2,1)S(1)}, u32[]{:S(2)}, u32[]{:S(2)}) async-start(bf16[32,32,512]{2,1,0:T(8,128)(2,1)} %precondition.1), calls=%async_computation.1 | async-start | bytes 2097152 | tf_op jit(solution)/shard_map/all_to_all | solution.py:238
  68.7 0.0 copy-start.3
  68.7 3.9 %fusion = f32[1,1,2,512,512]{4,3,2,1,0:T(8,128)} fusion(f32[1,1,2,512,512]{4,3,2,1,0:T(8,128)} %param.13, bf16[2,512,512]{2,1,0:T(8,128)(2,1)S(1)} %bitcast.22), kind=kOutput, calls=%fused_computation.1 | convolution fusion | flops 538443776 | bytes 5242880 | tf_op jit(solution)/shard_map/vmap()/dot_general | solution.py:189
  72.6 0.0 copy-done.3
  72.6 2.1 %fusion.1 = f32[1,1,2,512,512]{4,3,2,1,0:T(8,128)} fusion(f32[1,1,2,512,512]{4,3,2,1,0:T(8,128)S(1)} %copy-done.3, bf16[2,512,512]{2,1,0:T(8,128)(2,1)S(1)} %bitcast.23), kind=kOutput, calls=%fused_computation.3 | convolution fusion | flops 538443776 | bytes 5242880 | tf_op jit(solution)/shard_map/vmap()/dot_general | solution.py:186
  74.7 16.2 %all-to-all-done.1.returned = bf16[32,32,512]{2,1,0:T(8,128)(2,1)S(1)} async-done(((bf16[32,32,512]{2,1,0:T(8,128)(2,1)}), bf16[32,32,512]{2,1,0:T(8,128)(2,1)S(1)}, u32[]{:S(2)}, u32[]{:S(2)}) %all-to-all-start.1) | async-done | bytes 1048608 | tf_op jit(solution)/shard_map/all_to_all | solution.py:238
  91.0 1.3 %collect.1 = bf16[32,3584]{1,0:T(8,128)(2,1)} custom-call(s32[7]{0:T(128)S(1)} %dynamic-slice_bitcast_fusion.owners, bf16[32,32,512]{2,1,0:T(8,128)(2,1)S(1)} %all-to-all-done.1.returned), custom_call_target="tpu_custom_call" | custom-call | tf_op jit(solution)/shard_map/collect/pallas_call | solution.py:172
  (3 shorter events, 0.1 us)
Async XLA Ops:
  0.6 18.4 %copy-start = (s32[2,56]{1,0:T(2,128)S(1)}, s32[2,56]{1,0:T(2,128)}, u32[]{:S(2)}) copy-start(s32[2,56]{1,0:T(2,128)} %param.11) | copy-start | bytes 1348
  2.0 5.4 %collective-permute-start.6 = (bf16[4,32,3584]{2,1,0:T(8,128)(2,1)S(1)}, bf16[4,32,3584]{2,1,0:T(8,128)(2,1)S(1)}, u32[]{:S(2)}, u32[]{:S(2)}) collective-permute-start(bf16[4,32,3584]{2,1,0:T(8,128)(2,1)S(1)} %groups.3), channel_id=1, source_target_pairs={{0,1},{1,0},{2,3},{3,2},{4,5},{5,4},{6,7},{7,6},{8,9},{9,8},{10,11... | collective-permute-start | bytes 2752520 | tf_op jit(solution)/shard_map/ppermute | solution.py:211
  8.3 11.6 %collective-permute-start.7 = (bf16[16,128]{1,0:T(8,128)(2,1)S(1)}, bf16[16,128]{1,0:T(8,128)(2,1)S(1)}, u32[]{:S(2)}, u32[]{:S(2)}) collective-permute-start(bf16[16,128]{1,0:T(8,128)(2,1)S(1)} %get-tuple-element.54), channel_id=1, source_target_pairs={{0,1},{1,0},{2,3},{3,2},{4,5},{5,4},{6,7},{7,6},{8,9},{9,8},{10,11... | collective-permute-start | bytes 12296 | tf_op jit(solution)/shard_map/ppermute | solution.py:227
  19.9 40.8 %copy-start.1 = (bf16[1,1,2,512,512]{4,3,2,1,0:T(8,128)(2,1)S(1)}, bf16[1,1,2,512,512]{4,3,2,1,0:T(8,128)(2,1)}, u32[]{:S(2)}) copy-start(bf16[1,1,2,512,512]{4,3,2,1,0:T(8,128)(2,1)} %param.14) | copy-start | bytes 3145732
  19.9 40.8 %copy-start.2 = (bf16[1,1,2,512,512]{4,3,2,1,0:T(8,128)(2,1)S(1)}, bf16[1,1,2,512,512]{4,3,2,1,0:T(8,128)(2,1)}, u32[]{:S(2)}) copy-start(bf16[1,1,2,512,512]{4,3,2,1,0:T(8,128)(2,1)} %param.15) | copy-start | bytes 3145732
  19.9 6.7 %collective-permute-start.3 = (bf16[32,3584]{1,0:T(8,128)(2,1)}, bf16[32,3584]{1,0:T(8,128)(2,1)S(1)}, u32[]{:S(2)}, u32[]{:S(2)}) collective-permute-start(bf16[32,3584]{1,0:T(8,128)(2,1)} %get-tuple-element.36), channel_id=1, source_target_pairs={{0,4},{1,5},{2,6},{3,7},{4,0},{5,1},{6,2},{7,3},{8,12},{9,13},{10,... | collective-permute-start | bytes 688136 | tf_op jit(solution)/shard_map/cond/branch_1_fun/ppermute | solution.py:216
  21.1 7.9 %collective-permute-start.4 = (bf16[32,3584]{1,0:T(8,128)(2,1)S(1)}, bf16[32,3584]{1,0:T(8,128)(2,1)S(1)}, u32[]{:S(2)}, u32[]{:S(2)}) collective-permute-start(bf16[32,3584]{1,0:T(8,128)(2,1)S(1)} %get-tuple-element.37), channel_id=1, source_target_pairs={{0,2},{1,3},{2,4},{3,5},{4,6},{5,7},{6,0},{7,1},{8,10},{9,11},{10,... | collective-permute-start | bytes 688136 | tf_op jit(solution)/shard_map/cond/branch_1_fun/ppermute | solution.py:216
  22.1 6.8 %collective-permute-start.5 = (bf16[32,3584]{1,0:T(8,128)(2,1)}, bf16[32,3584]{1,0:T(8,128)(2,1)S(1)}, u32[]{:S(2)}, u32[]{:S(2)}) collective-permute-start(bf16[32,3584]{1,0:T(8,128)(2,1)} %get-tuple-element.38), channel_id=1, source_target_pairs={{0,6},{1,7},{2,0},{3,1},{4,2},{5,3},{6,4},{7,5},{8,14},{9,15},{10,... | collective-permute-start | bytes 688136 | tf_op jit(solution)/shard_map/cond/branch_1_fun/ppermute | solution.py:216
  63.5 27.5 %all-to-all-start.1 = ((bf16[32,32,512]{2,1,0:T(8,128)(2,1)}), bf16[32,32,512]{2,1,0:T(8,128)(2,1)S(1)}, u32[]{:S(2)}, u32[]{:S(2)}) async-start(bf16[32,32,512]{2,1,0:T(8,128)(2,1)} %precondition.1), calls=%async_computation.1 | async-start | bytes 2097152 | tf_op jit(solution)/shard_map/all_to_all | solution.py:238
  68.7 3.9 %copy-start.3 = (f32[1,1,2,512,512]{4,3,2,1,0:T(8,128)S(1)}, f32[1,1,2,512,512]{4,3,2,1,0:T(8,128)}, u32[]{:S(2)}) copy-start(f32[1,1,2,512,512]{4,3,2,1,0:T(8,128)} %param.12) | copy-start | bytes 6291460

commit v4 on v3

--- a/solution.py
+++ b/solution.py
@@ -9,7 +9,7 @@
 
 BETA = 0.9
 EPS = 1e-06
-TOKEN = (16, 128)
+RING_ROWS = 16
 Y_ORDER = (2, 1, 3)
 VMEM_LIMIT = 24 * 1024 * 1024
 ANY = pl.BlockSpec(memory_space=pl.ANY)
@@ -83,26 +83,75 @@
 
 
 def total_kernel(block, *refs):
-    out, token = refs[-2:]
+    out = refs[-1]
     for c in range(out.shape[1] // block):
         columns = slice(c * block, (c + 1) * block)
-        out[:, columns] = total_of(refs[:-2], columns)
-    token[...] = jnp.zeros_like(token)
+        out[:, columns] = total_of(refs[:-1], columns)
 
 
 def add_up(parts, block):
     return pl.pallas_call(
         functools.partial(total_kernel, block),
-        out_shape=[
-            jax.ShapeDtypeStruct(parts[0].shape, jnp.bfloat16),
-            jax.ShapeDtypeStruct(TOKEN, jnp.bfloat16),
-        ],
+        out_shape=jax.ShapeDtypeStruct(parts[0].shape, jnp.bfloat16),
         in_specs=[VMEM] * len(parts),
-        out_specs=[VMEM] * 2,
+        out_specs=VMEM,
         compiler_params=params(),
         cost_estimate=CHEAP,
         name="add_up",
     )(*parts)
+
+
+def rows_kernel(start, rows, part, *refs):
+    out = refs[-1]
+    out[...] = part[start : start + rows]
+
+
+def take_rows(part, start, rows, *after):
+    return pl.pallas_call(
+        functools.partial(rows_kernel, start, rows),
+        out_shape=jax.ShapeDtypeStruct((rows, part.shape[1]), part.dtype),
+        in_specs=[VMEM] + [ANY] * len(after),
+        out_specs=VMEM,
+        compiler_params=params(),
+        cost_estimate=CHEAP,
+        name="take_rows",
+    )(part, *after)
+
+
+def plus_kernel(start, part, running, out):
+    out[...] = part[start : start + running.shape[0]] + running[...]
+
+
+def plus(part, start, running):
+    return pl.pallas_call(
+        functools.partial(plus_kernel, start),
+        out_shape=jax.ShapeDtypeStruct(running.shape, running.dtype),
+        in_specs=[VMEM] * 2,
+        out_specs=VMEM,
+        compiler_params=params(),
+        cost_estimate=CHEAP,
+        name="plus",
+    )(part, running)
+
+
+def join_kernel(*refs):
+    start = 0
+    for ref in refs[:-1]:
+        refs[-1][start : start + ref.shape[0]] = ref[...]
+        start += ref.shape[0]
+
+
+def join(pieces):
+    rows = sum(piece.shape[0] for piece in pieces)
+    return pl.pallas_call(
+        join_kernel,
+        out_shape=jax.ShapeDtypeStruct((rows, pieces[0].shape[1]), pieces[0].dtype),
+        in_specs=[VMEM] * len(pieces),
+        out_specs=VMEM,
+        compiler_params=params(),
+        cost_estimate=CHEAP,
+        name="join",
+    )(*pieces)
 
 
 def slots_kernel(pieces, block, n_parts, owners, *refs):
@@ -206,33 +255,26 @@
         owner, (fsdp_index * strip // block, rep_index * pieces), (1, pieces)
     )[0]
 
-    core = rep_index % 2
     swap = [(i, i + 1 - 2 * (i % 2)) for i in range(n_rep)]
     other = lax.ppermute(groups(grads[0], ring, width, True), "rep", swap)
     parts = pair_sum(groups(grads[0], ring, width, False), other)
 
-    def along_y(parts):
-        arrived = [
-            lax.ppermute(parts[step], "rep", [(i, (i + 2 * step) % n_rep) for i in range(n_rep)])
-            for step in Y_ORDER
-        ]
-        return [parts[0], *arrived]
-
-    total, token = lax.cond(
-        core == 0,
-        lambda parts: tuple(add_up(along_y(parts), block)),
-        lambda parts: (parts[0], jnp.zeros(TOKEN, jnp.bfloat16)),
-        parts,
-    )
-    token = lax.ppermute(token, "rep", swap)
-    outgoing = lax.cond(
-        core == 1,
-        lambda parts, total, token, owners: fill_slots(
-            along_y(parts), owners, n_fsdp, block, token
-        ),
-        lambda parts, total, token, owners: fill_slots([total], owners, n_fsdp, block),
-        parts, total, token, owners,
-    )
+    def send_y(array, step):
+        return lax.ppermute(array, "rep", [(i, (i + 2 * step) % n_rep) for i in range(n_rep)])
+
+    def directly(parts):
+        return add_up([parts[0]] + [send_y(parts[step], step) for step in Y_ORDER], block)
+
+    def round_ring(parts):
+        running = take_rows(parts[-1], 0, RING_ROWS)
+        for part in parts[-2::-1]:
+            running = plus(part, 0, send_y(running, 1))
+        rest = [take_rows(part, RING_ROWS, strip - RING_ROWS, running) for part in parts]
+        rest = add_up([rest[0]] + [send_y(rest[step], step) for step in Y_ORDER], block)
+        return join([running, rest])
+
+    total = lax.cond(rep_index % 2 == 0, directly, round_ring, parts)
+    outgoing = fill_slots([total], owners, n_fsdp, block)
     incoming = lax.all_to_all(outgoing, "fsdp", split_axis=0, concat_axis=0, tiled=True)
     results = precondition(incoming, left_root[0, 0], right_root[0, 0])
     returned = lax.all_to_all(results, "fsdp", split_axis=0, concat_axis=0, tiled=True)

time: 92.6 us -> 89.6 us (0.968)
  starting transfers between devices: 23.1 us -> 11.1 us
  waiting for transfers between devices: 22.9 us -> 34.2 us
  Pallas kernels: 9.29 us -> 7.61 us
    ppermute x4 -> x6, waiting for transfers between devices: 5.94 us -> 19 us  [send_y(): lax.ppermute(array, 'rep', [(i, (i + 2 * step) % n_rep) for i in range(n_...]
    ppermute x4 -> x6, starting transfers between devices: 14.6 us -> 3.17 us  [send_y(): lax.ppermute(array, 'rep', [(i, (i + 2 * step) % n_rep) for i in range(n_...]
    all_to_all x1, waiting for transfers between devices: 16.2 us -> 14.5 us  [on_device(): lax.all_to_all(results, 'fsdp', split_axis=0, concat_axis=0, tiled=True)]
    pallas_call x1, Pallas kernels: 1.68 us -> 0.62 us  [fill_slots(): pl.pallas_call(functools.partial(slots_kernel, width // block, block, len...]
  transfers between devices with their start and end apart: 6 -> 8, of which waited for: 5 -> 7; matrix products, arithmetic and copies ran while one was open for 7% -> 7% of each run, Pallas kernels for 1% -> 1%
where the time goes in v4:
time: 89.6 us; the launch traced here: 89.3 us
  waiting for transfers between devices  34.2 us (38%)
  blocking collectives  29.5 us (33%)
  starting transfers between devices  11.1 us (12%)
  Pallas kernels  7.61 us (8%)
  matrix products  5.96 us (7%)
    all_to_all x1, blocking collectives, on_device(): lax.all_to_all(outgoing, 'fsdp', split_axis=0, concat_axis=0, tiled=True)  29.5 us
    ppermute x6, waiting for transfers between devices, send_y(): lax.ppermute(array, 'rep', [(i, (i + 2 * step) % n_rep) for i in range(n_...  19 us
    all_to_all x1, waiting for transfers between devices, on_device(): lax.all_to_all(results, 'fsdp', split_axis=0, concat_axis=0, tiled=True)  14.5 us
    all_to_all x1, starting transfers between devices, on_device(): lax.all_to_all(results, 'fsdp', split_axis=0, concat_axis=0, tiled=True)  4.64 us
    dot_general x1, matrix products, statistics(): lax.dot_general(g, g, (((0,), (0,)), ((), ())), preferred_element_type=jn...  3.88 us
    ppermute x1, starting transfers between devices, on_device(): other = lax.ppermute(groups(grads[0], ring, width, True), 'rep', swap)  3.33 us
    ppermute x6, starting transfers between devices, send_y(): lax.ppermute(array, 'rep', [(i, (i + 2 * step) % n_rep) for i in range(n_...  3.17 us
    pallas_call x1, Pallas kernels, precondition(): pl.pallas_call(precondition_kernel, out_shape=jax.ShapeDtypeStruct(incomi...  2.8 us
  transfers between devices with their start and end apart: 8, of which 7 were waited for; matrix products, arithmetic and copies ran while one was open for 7% of the time, Pallas kernels for 1%

profile of v4, /device:TPU:1, one launch (start us, length us, event | category | flops | bytes accessed | tf_op | source)
XLA Modules:
  0.0 89.3 jit_solution(5216822968484921718)
XLA Ops:
  0.6 0.0 copy-start
  0.6 1.3 %groups.3 = bf16[4,32,3584]{2,1,0:T(8,128)(2,1)S(1)} custom-call(bf16[32,28672]{1,0:T(8,128)(2,1)} %bitcast.26), custom_call_target="tpu_custom_call" | custom-call | flops 1 | bytes 2097152 | tf_op jit(solution)/shard_map/groups/pallas_call | solution.py:47
  2.0 3.3 %collective-permute-start.9 = (bf16[4,32,3584]{2,1,0:T(8,128)(2,1)S(1)}, bf16[4,32,3584]{2,1,0:T(8,128)(2,1)S(1)}, u32[]{:S(2)}, u32[]{:S(2)}) collective-permute-start(bf16[4,32,3584]{2,1,0:T(8,128)(2,1)S(1)} %groups.3), channel_id=1, source_target_pairs={{0,1},{1,0},{2,3},{3,2},{4,5},{5,4},{6,7},{7,6},{8,9},{9,8},{10,11... | collective-permute-start | bytes 2752520 | tf_op jit(solution)/shard_map/ppermute | solution.py:259
  5.3 1.3 %groups.2.kept = bf16[4,32,3584]{2,1,0:T(8,128)(2,1)S(1)} custom-call(bf16[32,28672]{1,0:T(8,128)(2,1)} %bitcast.27), custom_call_target="tpu_custom_call" | custom-call | flops 1 | bytes 2097152 | tf_op jit(solution)/shard_map/groups/pallas_call | solution.py:47
  6.7 0.0 copy-done
  6.7 0.1 dynamic-slice_bitcast_fusion.owners
  6.7 0.7 collective-permute-done.9.other
  7.4 0.1 pair_sum.1
  7.5 22.5 %conditional.1 = (bf16[32,3584]{1,0:T(8,128)(2,1)S(1)}) conditional(s32[]{:T(128)} %convert_element_type.3, (bf16[32,3584]{1,0:T(8,128)(2,1)S(1)}, bf16[32,3584]{1,0:T(8,128)(2,1)S(1)}, bf16[32,3584]{1,0:T(8,128)(2,1)S(1)}, bf16[32,3584]{1,0:T(8,128)(2,1)S(1)}) %tuple.14, (bf16[32,3584]{1,0:T(8,128)(2,1)S(1)}, bf16[32,3584]{1,0:T(8,128)(2,1)S(1)}, ...), branch_computations={%region_0.1_spmd, %region_1.2_spmd} | conditional | flops 10 | bytes 2752770 | solution.py:276
  7.5 0.1 collective-permute-start
  7.6 5.1 %collective-permute-done.running = bf16[16,3584]{1,0:T(8,128)(2,1)S(1)} collective-permute-done((bf16[16,3584]{1,0:T(8,128)(2,1)S(1)}, bf16[16,3584]{1,0:T(8,128)(2,1)S(1)}, u32[]{:S(2)}, u32[]{:S(2)}) %collective-permute-start) | collective-permute-done | bytes 114720 | tf_op jit(solution)/shard_map/cond/branch_0_fun/ppermute | solution.py:263
  12.8 0.1 collective-permute-start.1
  12.9 5.7 %collective-permute-done.1.running = bf16[16,3584]{1,0:T(8,128)(2,1)S(1)} collective-permute-done((bf16[16,3584]{1,0:T(8,128)(2,1)S(1)}, bf16[16,3584]{1,0:T(8,128)(2,1)S(1)}, u32[]{:S(2)}, u32[]{:S(2)}) %collective-permute-start.1) | collective-permute-done | bytes 114720 | tf_op jit(solution)/shard_map/cond/branch_0_fun/ppermute | solution.py:263
  18.6 0.1 collective-permute-start.2
  18.7 4.8 %collective-permute-done.2.running = bf16[16,3584]{1,0:T(8,128)(2,1)S(1)} collective-permute-done((bf16[16,3584]{1,0:T(8,128)(2,1)S(1)}, bf16[16,3584]{1,0:T(8,128)(2,1)S(1)}, u32[]{:S(2)}, u32[]{:S(2)}) %collective-permute-start.2) | collective-permute-done | bytes 114720 | tf_op jit(solution)/shard_map/cond/branch_0_fun/ppermute | solution.py:263
  23.6 0.1 collective-permute-start.3
  23.7 0.2 collective-permute-start.4
  23.9 2.6 %collective-permute-start.5 = (bf16[16,3584]{1,0:T(8,128)(2,1)S(1)}, bf16[16,3584]{1,0:T(8,128)(2,1)S(1)}, u32[]{:S(2)}, u32[]{:S(2)}) collective-permute-start(bf16[16,3584]{1,0:T(8,128)(2,1)S(1)} %take_rows.9), channel_id=1, source_target_pairs={{0,6},{1,7},{2,0},{3,1},{4,2},{5,3},{6,4},{7,5},{8,14},{9,15},{10,... | collective-permute-start | bytes 344072 | tf_op jit(solution)/shard_map/cond/branch_0_fun/ppermute | solution.py:263
  26.6 2.4 %collective-permute-done.3.refs_1_ = bf16[16,3584]{1,0:T(8,128)(2,1)S(1)} collective-permute-done((bf16[16,3584]{1,0:T(8,128)(2,1)S(1)}, bf16[16,3584]{1,0:T(8,128)(2,1)S(1)}, u32[]{:S(2)}, u32[]{:S(2)}) %collective-permute-start.3) | collective-permute-done | bytes 114720 | tf_op jit(solution)/shard_map/cond/branch_0_fun/ppermute | solution.py:263
  29.0 0.9 %collective-permute-done.4.refs_2_ = bf16[16,3584]{1,0:T(8,128)(2,1)S(1)} collective-permute-done((bf16[16,3584]{1,0:T(8,128)(2,1)S(1)}, bf16[16,3584]{1,0:T(8,128)(2,1)S(1)}, u32[]{:S(2)}, u32[]{:S(2)}) %collective-permute-start.4) | collective-permute-done | bytes 114720 | tf_op jit(solution)/shard_map/cond/branch_0_fun/ppermute | solution.py:263
  29.9 0.0 collective-permute-done.5.refs_3_
  29.9 0.1 add_up.2.refs_1_
  30.0 0.0 copy-start.1
  30.0 0.0 copy-start.2
  30.0 0.6 fill_slots.1
  30.6 29.5 %all_to_all.10.g_ref = bf16[32,32,512]{2,1,0:T(8,128)(2,1)S(1)} all-to-all(bf16[32,32,512]{2,1,0:T(8,128)(2,1)S(1)} %fill_slots.1), channel_id=1, replica_groups=mesh['fsdp'=32,'rep'=8] {'fsdp'}, dimensions={0} | all-to-all | bytes 2097152 | tf_op jit(solution)/shard_map/all_to_all | solution.py:278
  60.1 0.0 copy-done.1
  60.1 0.0 copy-done.2
  60.1 2.8 %precondition.1 = bf16[32,32,512]{2,1,0:T(8,128)(2,1)} custom-call(bf16[32,32,512]{2,1,0:T(8,128)(2,1)S(1)} %all_to_all.10.g_ref, bf16[2,512,512]{2,1,0:T(8,128)(2,1)S(1)} %bitcast.24, bf16[2,512,512]{2,1,0:T(8,128)(2,1)S(1)} %bitcast.25), custom_call_target="tpu_custom_call" | custom-call | flops 1073741824 | bytes 4194304 | tf_op jit(solution)/shard_map/precondition/pallas_call | solution.py:193
  62.9 4.6 %all-to-all-start.1 = ((bf16[32,32,512]{2,1,0:T(8,128)(2,1)}), bf16[32,32,512]{2,1,0:T(8,128)(2,1)S(1)}, u32[]{:S(2)}, u32[]{:S(2)}) async-start(bf16[32,32,512]{2,1,0:T(8,128)(2,1)} %precondition.1), calls=%async_computation.1 | async-start | bytes 2097152 | tf_op jit(solution)/shard_map/all_to_all | solution.py:280
  67.6 0.0 copy-start.3
  67.6 3.9 %fusion = f32[1,1,2,512,512]{4,3,2,1,0:T(8,128)} fusion(f32[1,1,2,512,512]{4,3,2,1,0:T(8,128)} %param.11, bf16[2,512,512]{2,1,0:T(8,128)(2,1)S(1)} %bitcast.22), kind=kOutput, calls=%fused_computation.1 | convolution fusion | flops 538443776 | bytes 5242880 | tf_op jit(solution)/shard_map/vmap()/dot_general | solution.py:238
  71.5 0.0 copy-done.3
  71.5 2.1 %fusion.1 = f32[1,1,2,512,512]{4,3,2,1,0:T(8,128)} fusion(f32[1,1,2,512,512]{4,3,2,1,0:T(8,128)S(1)} %copy-done.3, bf16[2,512,512]{2,1,0:T(8,128)(2,1)S(1)} %bitcast.23), kind=kOutput, calls=%fused_computation.3 | convolution fusion | flops 538443776 | bytes 5242880 | tf_op jit(solution)/shard_map/vmap()/dot_general | solution.py:235
  73.5 14.5 %all-to-all-done.1.returned = bf16[32,32,512]{2,1,0:T(8,128)(2,1)S(1)} async-done(((bf16[32,32,512]{2,1,0:T(8,128)(2,1)}), bf16[32,32,512]{2,1,0:T(8,128)(2,1)S(1)}, u32[]{:S(2)}, u32[]{:S(2)}) %all-to-all-start.1) | async-done | bytes 1048608 | tf_op jit(solution)/shard_map/all_to_all | solution.py:280
  88.0 1.3 %collect.1 = bf16[32,3584]{1,0:T(8,128)(2,1)} custom-call(s32[7]{0:T(128)S(1)} %dynamic-slice_bitcast_fusion.owners, bf16[32,32,512]{2,1,0:T(8,128)(2,1)S(1)} %all-to-all-done.1.returned), custom_call_target="tpu_custom_call" | custom-call | tf_op jit(solution)/shard_map/collect/pallas_call | solution.py:221
  (9 shorter events, 0.1 us)
Async XLA Ops:
  0.6 6.0 %copy-start = (s32[2,56]{1,0:T(2,128)S(1)}, s32[2,56]{1,0:T(2,128)}, u32[]{:S(2)}) copy-start(s32[2,56]{1,0:T(2,128)} %param.9) | copy-start | bytes 1348
  2.0 5.4 %collective-permute-start.9 = (bf16[4,32,3584]{2,1,0:T(8,128)(2,1)S(1)}, bf16[4,32,3584]{2,1,0:T(8,128)(2,1)S(1)}, u32[]{:S(2)}, u32[]{:S(2)}) collective-permute-start(bf16[4,32,3584]{2,1,0:T(8,128)(2,1)S(1)} %groups.3), channel_id=1, source_target_pairs={{0,1},{1,0},{2,3},{3,2},{4,5},{5,4},{6,7},{7,6},{8,9},{9,8},{10,11... | collective-permute-start | bytes 2752520 | tf_op jit(solution)/shard_map/ppermute | solution.py:259
  7.5 5.2 %collective-permute-start = (bf16[16,3584]{1,0:T(8,128)(2,1)S(1)}, bf16[16,3584]{1,0:T(8,128)(2,1)S(1)}, u32[]{:S(2)}, u32[]{:S(2)}) collective-permute-start(bf16[16,3584]{1,0:T(8,128)(2,1)S(1)} %take_rows.5), channel_id=1, source_target_pairs={{0,2},{1,3},{2,4},{3,5},{4,6},{5,7},{6,0},{7,1},{8,10},{9,11},{10,... | collective-permute-start | bytes 344072 | tf_op jit(solution)/shard_map/cond/branch_0_fun/ppermute | solution.py:263
  12.8 5.8 %collective-permute-start.1 = (bf16[16,3584]{1,0:T(8,128)(2,1)S(1)}, bf16[16,3584]{1,0:T(8,128)(2,1)S(1)}, u32[]{:S(2)}, u32[]{:S(2)}) collective-permute-start(bf16[16,3584]{1,0:T(8,128)(2,1)S(1)} %plus.3), channel_id=1, source_target_pairs={{0,2},{1,3},{2,4},{3,5},{4,6},{5,7},{6,0},{7,1},{8,10},{9,11},{10,... | collective-permute-start | bytes 344072 | tf_op jit(solution)/shard_map/cond/branch_0_fun/ppermute | solution.py:263
  18.6 4.9 %collective-permute-start.2 = (bf16[16,3584]{1,0:T(8,128)(2,1)S(1)}, bf16[16,3584]{1,0:T(8,128)(2,1)S(1)}, u32[]{:S(2)}, u32[]{:S(2)}) collective-permute-start(bf16[16,3584]{1,0:T(8,128)(2,1)S(1)} %plus.4), channel_id=1, source_target_pairs={{0,2},{1,3},{2,4},{3,5},{4,6},{5,7},{6,0},{7,1},{8,10},{9,11},{10,... | collective-permute-start | bytes 344072 | tf_op jit(solution)/shard_map/cond/branch_0_fun/ppermute | solution.py:263
  23.6 5.3 %collective-permute-start.3 = (bf16[16,3584]{1,0:T(8,128)(2,1)S(1)}, bf16[16,3584]{1,0:T(8,128)(2,1)S(1)}, u32[]{:S(2)}, u32[]{:S(2)}) collective-permute-start(bf16[16,3584]{1,0:T(8,128)(2,1)S(1)} %take_rows.7), channel_id=1, source_target_pairs={{0,4},{1,5},{2,6},{3,7},{4,0},{5,1},{6,2},{7,3},{8,12},{9,13},{10,... | collective-permute-start | bytes 344072 | tf_op jit(solution)/shard_map/cond/branch_0_fun/ppermute | solution.py:263
  23.7 6.2 %collective-permute-start.4 = (bf16[16,3584]{1,0:T(8,128)(2,1)S(1)}, bf16[16,3584]{1,0:T(8,128)(2,1)S(1)}, u32[]{:S(2)}, u32[]{:S(2)}) collective-permute-start(bf16[16,3584]{1,0:T(8,128)(2,1)S(1)} %take_rows.8), channel_id=1, source_target_pairs={{0,2},{1,3},{2,4},{3,5},{4,6},{5,7},{6,0},{7,1},{8,10},{9,11},{10,... | collective-permute-start | bytes 344072 | tf_op jit(solution)/shard_map/cond/branch_0_fun/ppermute | solution.py:263
  23.9 6.0 %collective-permute-start.5 = (bf16[16,3584]{1,0:T(8,128)(2,1)S(1)}, bf16[16,3584]{1,0:T(8,128)(2,1)S(1)}, u32[]{:S(2)}, u32[]{:S(2)}) collective-permute-start(bf16[16,3584]{1,0:T(8,128)(2,1)S(1)} %take_rows.9), channel_id=1, source_target_pairs={{0,6},{1,7},{2,0},{3,1},{4,2},{5,3},{6,4},{7,5},{8,14},{9,15},{10,... | collective-permute-start | bytes 344072 | tf_op jit(solution)/shard_map/cond/branch_0_fun/ppermute | solution.py:263
  30.0 30.1 %copy-start.1 = (bf16[1,1,2,512,512]{4,3,2,1,0:T(8,128)(2,1)S(1)}, bf16[1,1,2,512,512]{4,3,2,1,0:T(8,128)(2,1)}, u32[]{:S(2)}) copy-start(bf16[1,1,2,512,512]{4,3,2,1,0:T(8,128)(2,1)} %param.12) | copy-start | bytes 3145732
  30.0 30.1 %copy-start.2 = (bf16[1,1,2,512,512]{4,3,2,1,0:T(8,128)(2,1)S(1)}, bf16[1,1,2,512,512]{4,3,2,1,0:T(8,128)(2,1)}, u32[]{:S(2)}) copy-start(bf16[1,1,2,512,512]{4,3,2,1,0:T(8,128)(2,1)} %param.13) | copy-start | bytes 3145732
  62.9 25.1 %all-to-all-start.1 = ((bf16[32,32,512]{2,1,0:T(8,128)(2,1)}), bf16[32,32,512]{2,1,0:T(8,128)(2,1)S(1)}, u32[]{:S(2)}, u32[]{:S(2)}) async-start(bf16[32,32,512]{2,1,0:T(8,128)(2,1)} %precondition.1), calls=%async_computation.1 | async-start | bytes 2097152 | tf_op jit(solution)/shard_map/all_to_all | solution.py:280
  67.6 3.9 %copy-start.3 = (f32[1,1,2,512,512]{4,3,2,1,0:T(8,128)S(1)}, f32[1,1,2,512,512]{4,3,2,1,0:T(8,128)}, u32[]{:S(2)}) copy-start(f32[1,1,2,512,512]{4,3,2,1,0:T(8,128)} %param.10) | copy-start | bytes 6291460

commit v5 on v4

--- a/solution.py
+++ b/solution.py
@@ -9,7 +9,6 @@
 
 BETA = 0.9
 EPS = 1e-06
-RING_ROWS = 16
 Y_ORDER = (2, 1, 3)
 VMEM_LIMIT = 24 * 1024 * 1024
 ANY = pl.BlockSpec(memory_space=pl.ANY)
@@ -101,30 +100,30 @@
     )(*parts)
 
 
-def rows_kernel(start, rows, part, *refs):
+def take_kernel(start, part, *refs):
     out = refs[-1]
-    out[...] = part[start : start + rows]
-
-
-def take_rows(part, start, rows, *after):
-    return pl.pallas_call(
-        functools.partial(rows_kernel, start, rows),
-        out_shape=jax.ShapeDtypeStruct((rows, part.shape[1]), part.dtype),
+    out[...] = part[:, start : start + out.shape[1]]
+
+
+def take(part, start, stop, *after):
+    return pl.pallas_call(
+        functools.partial(take_kernel, start),
+        out_shape=jax.ShapeDtypeStruct((part.shape[0], stop - start), part.dtype),
         in_specs=[VMEM] + [ANY] * len(after),
         out_specs=VMEM,
         compiler_params=params(),
         cost_estimate=CHEAP,
-        name="take_rows",
+        name="take",
     )(part, *after)
 
 
-def plus_kernel(start, part, running, out):
-    out[...] = part[start : start + running.shape[0]] + running[...]
-
-
-def plus(part, start, running):
-    return pl.pallas_call(
-        functools.partial(plus_kernel, start),
+def plus_kernel(part, running, out):
+    out[...] = part[:, : running.shape[1]] + running[...]
+
+
+def plus(part, running):
+    return pl.pallas_call(
+        plus_kernel,
         out_shape=jax.ShapeDtypeStruct(running.shape, running.dtype),
         in_specs=[VMEM] * 2,
         out_specs=VMEM,
@@ -137,15 +136,15 @@
 def join_kernel(*refs):
     start = 0
     for ref in refs[:-1]:
-        refs[-1][start : start + ref.shape[0]] = ref[...]
-        start += ref.shape[0]
+        refs[-1][:, start : start + ref.shape[1]] = ref[...]
+        start += ref.shape[1]
 
 
 def join(pieces):
-    rows = sum(piece.shape[0] for piece in pieces)
+    width = sum(piece.shape[1] for piece in pieces)
     return pl.pallas_call(
         join_kernel,
-        out_shape=jax.ShapeDtypeStruct((rows, pieces[0].shape[1]), pieces[0].dtype),
+        out_shape=jax.ShapeDtypeStruct((pieces[0].shape[0], width), pieces[0].dtype),
         in_specs=[VMEM] * len(pieces),
         out_specs=VMEM,
         compiler_params=params(),
@@ -266,10 +265,11 @@
         return add_up([parts[0]] + [send_y(parts[step], step) for step in Y_ORDER], block)
 
     def round_ring(parts):
-        running = take_rows(parts[-1], 0, RING_ROWS)
-        for part in parts[-2::-1]:
-            running = plus(part, 0, send_y(running, 1))
-        rest = [take_rows(part, RING_ROWS, strip - RING_ROWS, running) for part in parts]
+        running = take(parts[0], 0, block)
+        for part in parts[:0:-1]:
+            running = plus(part, send_y(running, 1))
+        running = send_y(running, 1)
+        rest = [take(part, block, width, running) for part in parts]
         rest = add_up([rest[0]] + [send_y(rest[step], step) for step in Y_ORDER], block)
         return join([running, rest])
 

time: 89.6 us -> 86.7 us (0.968)
  the two profiles are of different devices: /device:TPU:1 before, /device:TPU:33 now
where the time goes in v5:
time: 86.7 us; the launch traced here: 86.5 us
  waiting for transfers between devices  33.4 us (39%)
  blocking collectives  28.9 us (33%)
  starting transfers between devices  9.69 us (11%)
  Pallas kernels  7.65 us (9%)
  matrix products  5.95 us (7%)
    all_to_all x1, blocking collectives, on_device(): lax.all_to_all(outgoing, 'fsdp', split_axis=0, concat_axis=0, tiled=True)  28.9 us
    ppermute x7, waiting for transfers between devices, send_y(): lax.ppermute(array, 'rep', [(i, (i + 2 * step) % n_rep) for i in range(n_...  20.3 us
    all_to_all x1, waiting for transfers between devices, on_device(): lax.all_to_all(results, 'fsdp', split_axis=0, concat_axis=0, tiled=True)  12.4 us
    ppermute x7, starting transfers between devices, send_y(): lax.ppermute(array, 'rep', [(i, (i + 2 * step) % n_rep) for i in range(n_...  4.48 us
    all_to_all x1, starting transfers between devices, on_device(): lax.all_to_all(results, 'fsdp', split_axis=0, concat_axis=0, tiled=True)  4.45 us
    dot_general x1, matrix products, statistics(): lax.dot_general(g, g, (((0,), (0,)), ((), ())), preferred_element_type=jn...  3.88 us
    pallas_call x1, Pallas kernels, precondition(): pl.pallas_call(precondition_kernel, out_shape=jax.ShapeDtypeStruct(incomi...  2.82 us
    pallas_call x2, Pallas kernels, groups(): pl.pallas_call(functools.partial(groups_kernel, ring, width, other), out_...  2.65 us
  transfers between devices with their start and end apart: 9, of which 8 were waited for; matrix products, arithmetic and copies ran while one was open for 7% of the time, Pallas kernels for 2%

profile of v5, /device:TPU:33, one launch (start us, length us, event | category | flops | bytes accessed | tf_op | source)
XLA Modules:
  0.0 86.5 jit_solution(17747384566489545944)
XLA Ops:
  0.6 0.0 copy-start
  0.6 1.3 %groups.3 = bf16[4,32,3584]{2,1,0:T(8,128)(2,1)S(1)} custom-call(bf16[32,28672]{1,0:T(8,128)(2,1)} %bitcast.26), custom_call_target="tpu_custom_call" | custom-call | flops 1 | bytes 2097152 | tf_op jit(solution)/shard_map/groups/pallas_call | solution.py:46
  2.0 0.8 collective-permute-start.10
  2.7 1.3 %groups.2.kept = bf16[4,32,3584]{2,1,0:T(8,128)(2,1)S(1)} custom-call(bf16[32,28672]{1,0:T(8,128)(2,1)} %bitcast.27), custom_call_target="tpu_custom_call" | custom-call | flops 1 | bytes 2097152 | tf_op jit(solution)/shard_map/groups/pallas_call | solution.py:46
  4.1 0.0 copy-done
  4.1 0.1 dynamic-slice_bitcast_fusion.owners
  4.2 0.7 collective-permute-done.10.other
  4.8 0.1 pair_sum.1
  4.9 25.1 %conditional.1 = (bf16[32,3584]{1,0:T(8,128)(2,1)S(1)}) conditional(s32[]{:T(128)} %convert_element_type.3, (bf16[32,3584]{1,0:T(8,128)(2,1)S(1)}, bf16[32,3584]{1,0:T(8,128)(2,1)S(1)}, bf16[32,3584]{1,0:T(8,128)(2,1)S(1)}, bf16[32,3584]{1,0:T(8,128)(2,1)S(1)}) %tuple.14, (bf16[32,3584]{1,0:T(8,128)(2,1)S(1)}, bf16[32,3584]{1,0:T(8,128)(2,1)S(1)}, ...), branch_computations={%region_0.1_spmd, %region_1.2_spmd} | conditional | flops 10 | bytes 2883882 | solution.py:276
  5.0 1.4 %collective-permute-start = (bf16[32,512]{1,0:T(8,128)(2,1)S(1)}, bf16[32,512]{1,0:T(8,128)(2,1)S(1)}, u32[]{:S(2)}, u32[]{:S(2)}) collective-permute-start(bf16[32,512]{1,0:T(8,128)(2,1)S(1)} %take.5), channel_id=1, source_target_pairs={{0,2},{1,3},{2,4},{3,5},{4,6},{5,7},{6,0},{7,1},{8,10},{9,11},{10,... | collective-permute-start | bytes 98312 | tf_op jit(solution)/shard_map/cond/branch_0_fun/ppermute | solution.py:262
  6.3 2.7 %collective-permute-done.running = bf16[32,512]{1,0:T(8,128)(2,1)S(1)} collective-permute-done((bf16[32,512]{1,0:T(8,128)(2,1)S(1)}, bf16[32,512]{1,0:T(8,128)(2,1)S(1)}, u32[]{:S(2)}, u32[]{:S(2)}) %collective-permute-start) | collective-permute-done | bytes 32800 | tf_op jit(solution)/shard_map/cond/branch_0_fun/ppermute | solution.py:262
  9.1 0.0 collective-permute-start.1
  9.1 4.6 %collective-permute-done.1.running = bf16[32,512]{1,0:T(8,128)(2,1)S(1)} collective-permute-done((bf16[32,512]{1,0:T(8,128)(2,1)S(1)}, bf16[32,512]{1,0:T(8,128)(2,1)S(1)}, u32[]{:S(2)}, u32[]{:S(2)}) %collective-permute-start.1) | collective-permute-done | bytes 32800 | tf_op jit(solution)/shard_map/cond/branch_0_fun/ppermute | solution.py:262
  13.7 0.0 collective-permute-start.2
  13.7 4.0 %collective-permute-done.2.running = bf16[32,512]{1,0:T(8,128)(2,1)S(1)} collective-permute-done((bf16[32,512]{1,0:T(8,128)(2,1)S(1)}, bf16[32,512]{1,0:T(8,128)(2,1)S(1)}, u32[]{:S(2)}, u32[]{:S(2)}) %collective-permute-start.2) | collective-permute-done | bytes 32800 | tf_op jit(solution)/shard_map/cond/branch_0_fun/ppermute | solution.py:262
  17.7 0.0 collective-permute-start.3
  17.7 4.0 %collective-permute-done.3.refs_0_ = bf16[32,512]{1,0:T(8,128)(2,1)S(1)} collective-permute-done((bf16[32,512]{1,0:T(8,128)(2,1)S(1)}, bf16[32,512]{1,0:T(8,128)(2,1)S(1)}, u32[]{:S(2)}, u32[]{:S(2)}) %collective-permute-start.3) | collective-permute-done | bytes 32800 | tf_op jit(solution)/shard_map/cond/branch_0_fun/ppermute | solution.py:262
  21.7 0.2 collective-permute-start.4
  22.0 0.2 collective-permute-start.5
  22.2 2.6 %collective-permute-start.6 = (bf16[32,3072]{1,0:T(8,128)(2,1)S(1)}, bf16[32,3072]{1,0:T(8,128)(2,1)S(1)}, u32[]{:S(2)}, u32[]{:S(2)}) collective-permute-start(bf16[32,3072]{1,0:T(8,128)(2,1)S(1)} %take.9), channel_id=1, source_target_pairs={{0,6},{1,7},{2,0},{3,1},{4,2},{5,3},{6,4},{7,5},{8,14},{9,15},{10,... | collective-permute-start | bytes 589832 | tf_op jit(solution)/shard_map/cond/branch_0_fun/ppermute | solution.py:262
  24.8 3.1 %collective-permute-done.4.refs_1_ = bf16[32,3072]{1,0:T(8,128)(2,1)S(1)} collective-permute-done((bf16[32,3072]{1,0:T(8,128)(2,1)S(1)}, bf16[32,3072]{1,0:T(8,128)(2,1)S(1)}, u32[]{:S(2)}, u32[]{:S(2)}) %collective-permute-start.4) | collective-permute-done | bytes 196640 | tf_op jit(solution)/shard_map/cond/branch_0_fun/ppermute | solution.py:262
  27.9 2.0 %collective-permute-done.5.refs_2_ = bf16[32,3072]{1,0:T(8,128)(2,1)S(1)} collective-permute-done((bf16[32,3072]{1,0:T(8,128)(2,1)S(1)}, bf16[32,3072]{1,0:T(8,128)(2,1)S(1)}, u32[]{:S(2)}, u32[]{:S(2)}) %collective-permute-start.5) | collective-permute-done | bytes 196640 | tf_op jit(solution)/shard_map/cond/branch_0_fun/ppermute | solution.py:262
  29.9 0.0 collective-permute-done.6.refs_3_
  29.9 0.1 add_up.2.refs_1_
  30.0 0.0 copy-start.1
  30.0 0.0 copy-start.2
  30.0 0.6 fill_slots.1
  30.7 28.9 %all_to_all.10.g_ref = bf16[32,32,512]{2,1,0:T(8,128)(2,1)S(1)} all-to-all(bf16[32,32,512]{2,1,0:T(8,128)(2,1)S(1)} %fill_slots.1), channel_id=1, replica_groups=mesh['fsdp'=32,'rep'=8] {'fsdp'}, dimensions={0} | all-to-all | bytes 2097152 | tf_op jit(solution)/shard_map/all_to_all | solution.py:278
  59.6 0.0 copy-done.1
  59.6 0.0 copy-done.2
  59.6 2.8 %precondition.1 = bf16[32,32,512]{2,1,0:T(8,128)(2,1)} custom-call(bf16[32,32,512]{2,1,0:T(8,128)(2,1)S(1)} %all_to_all.10.g_ref, bf16[2,512,512]{2,1,0:T(8,128)(2,1)S(1)} %bitcast.24, bf16[2,512,512]{2,1,0:T(8,128)(2,1)S(1)} %bitcast.25), custom_call_target="tpu_custom_call" | custom-call | flops 1073741824 | bytes 4194304 | tf_op jit(solution)/shard_map/precondition/pallas_call | solution.py:192
  62.4 4.4 %all-to-all-start.1 = ((bf16[32,32,512]{2,1,0:T(8,128)(2,1)}), bf16[32,32,512]{2,1,0:T(8,128)(2,1)S(1)}, u32[]{:S(2)}, u32[]{:S(2)}) async-start(bf16[32,32,512]{2,1,0:T(8,128)(2,1)} %precondition.1), calls=%async_computation.1 | async-start | bytes 2097152 | tf_op jit(solution)/shard_map/all_to_all | solution.py:280
  66.8 0.0 copy-start.3
  66.8 3.9 %fusion = f32[1,1,2,512,512]{4,3,2,1,0:T(8,128)} fusion(f32[1,1,2,512,512]{4,3,2,1,0:T(8,128)} %param.11, bf16[2,512,512]{2,1,0:T(8,128)(2,1)S(1)} %bitcast.22), kind=kOutput, calls=%fused_computation.1 | convolution fusion | flops 538443776 | bytes 5242880 | tf_op jit(solution)/shard_map/vmap()/dot_general | solution.py:237
  70.7 0.0 copy-done.3
  70.7 2.1 %fusion.1 = f32[1,1,2,512,512]{4,3,2,1,0:T(8,128)} fusion(f32[1,1,2,512,512]{4,3,2,1,0:T(8,128)S(1)} %copy-done.3, bf16[2,512,512]{2,1,0:T(8,128)(2,1)S(1)} %bitcast.23), kind=kOutput, calls=%fused_computation.3 | convolution fusion | flops 538443776 | bytes 5242880 | tf_op jit(solution)/shard_map/vmap()/dot_general | solution.py:234
  72.8 12.4 %all-to-all-done.1.returned = bf16[32,32,512]{2,1,0:T(8,128)(2,1)S(1)} async-done(((bf16[32,32,512]{2,1,0:T(8,128)(2,1)}), bf16[32,32,512]{2,1,0:T(8,128)(2,1)S(1)}, u32[]{:S(2)}, u32[]{:S(2)}) %all-to-all-start.1) | async-done | bytes 1048608 | tf_op jit(solution)/shard_map/all_to_all | solution.py:280
  85.2 1.3 %collect.1 = bf16[32,3584]{1,0:T(8,128)(2,1)} custom-call(s32[7]{0:T(128)S(1)} %dynamic-slice_bitcast_fusion.owners, bf16[32,32,512]{2,1,0:T(8,128)(2,1)S(1)} %all-to-all-done.1.returned), custom_call_target="tpu_custom_call" | custom-call | tf_op jit(solution)/shard_map/collect/pallas_call | solution.py:220
  (9 shorter events, 0.1 us)
Async XLA Ops:
  0.6 3.5 %copy-start = (s32[2,56]{1,0:T(2,128)S(1)}, s32[2,56]{1,0:T(2,128)}, u32[]{:S(2)}) copy-start(s32[2,56]{1,0:T(2,128)} %param.9) | copy-start | bytes 1348
  2.0 2.9 %collective-permute-start.10 = (bf16[4,32,3584]{2,1,0:T(8,128)(2,1)S(1)}, bf16[4,32,3584]{2,1,0:T(8,128)(2,1)S(1)}, u32[]{:S(2)}, u32[]{:S(2)}) collective-permute-start(bf16[4,32,3584]{2,1,0:T(8,128)(2,1)S(1)} %groups.3), channel_id=1, source_target_pairs={{0,1},{1,0},{2,3},{3,2},{4,5},{5,4},{6,7},{7,6},{8,9},{9,8},{10,11... | collective-permute-start | bytes 2752520 | tf_op jit(solution)/shard_map/ppermute | solution.py:258
  5.0 4.1 %collective-permute-start = (bf16[32,512]{1,0:T(8,128)(2,1)S(1)}, bf16[32,512]{1,0:T(8,128)(2,1)S(1)}, u32[]{:S(2)}, u32[]{:S(2)}) collective-permute-start(bf16[32,512]{1,0:T(8,128)(2,1)S(1)} %take.5), channel_id=1, source_target_pairs={{0,2},{1,3},{2,4},{3,5},{4,6},{5,7},{6,0},{7,1},{8,10},{9,11},{10,... | collective-permute-start | bytes 98312 | tf_op jit(solution)/shard_map/cond/branch_0_fun/ppermute | solution.py:262
  9.1 4.6 %collective-permute-start.1 = (bf16[32,512]{1,0:T(8,128)(2,1)S(1)}, bf16[32,512]{1,0:T(8,128)(2,1)S(1)}, u32[]{:S(2)}, u32[]{:S(2)}) collective-permute-start(bf16[32,512]{1,0:T(8,128)(2,1)S(1)} %plus.3), channel_id=1, source_target_pairs={{0,2},{1,3},{2,4},{3,5},{4,6},{5,7},{6,0},{7,1},{8,10},{9,11},{10,... | collective-permute-start | bytes 98312 | tf_op jit(solution)/shard_map/cond/branch_0_fun/ppermute | solution.py:262
  13.7 4.0 %collective-permute-start.2 = (bf16[32,512]{1,0:T(8,128)(2,1)S(1)}, bf16[32,512]{1,0:T(8,128)(2,1)S(1)}, u32[]{:S(2)}, u32[]{:S(2)}) collective-permute-start(bf16[32,512]{1,0:T(8,128)(2,1)S(1)} %plus.4), channel_id=1, source_target_pairs={{0,2},{1,3},{2,4},{3,5},{4,6},{5,7},{6,0},{7,1},{8,10},{9,11},{10,... | collective-permute-start | bytes 98312 | tf_op jit(solution)/shard_map/cond/branch_0_fun/ppermute | solution.py:262
  17.7 4.0 %collective-permute-start.3 = (bf16[32,512]{1,0:T(8,128)(2,1)S(1)}, bf16[32,512]{1,0:T(8,128)(2,1)S(1)}, u32[]{:S(2)}, u32[]{:S(2)}) collective-permute-start(bf16[32,512]{1,0:T(8,128)(2,1)S(1)} %plus.5), channel_id=1, source_target_pairs={{0,2},{1,3},{2,4},{3,5},{4,6},{5,7},{6,0},{7,1},{8,10},{9,11},{10,... | collective-permute-start | bytes 98312 | tf_op jit(solution)/shard_map/cond/branch_0_fun/ppermute | solution.py:262
  21.7 6.2 %collective-permute-start.4 = (bf16[32,3072]{1,0:T(8,128)(2,1)S(1)}, bf16[32,3072]{1,0:T(8,128)(2,1)S(1)}, u32[]{:S(2)}, u32[]{:S(2)}) collective-permute-start(bf16[32,3072]{1,0:T(8,128)(2,1)S(1)} %take.7), channel_id=1, source_target_pairs={{0,4},{1,5},{2,6},{3,7},{4,0},{5,1},{6,2},{7,3},{8,12},{9,13},{10,... | collective-permute-start | bytes 589832 | tf_op jit(solution)/shard_map/cond/branch_0_fun/ppermute | solution.py:262
  22.0 7.9 %collective-permute-start.5 = (bf16[32,3072]{1,0:T(8,128)(2,1)S(1)}, bf16[32,3072]{1,0:T(8,128)(2,1)S(1)}, u32[]{:S(2)}, u32[]{:S(2)}) collective-permute-start(bf16[32,3072]{1,0:T(8,128)(2,1)S(1)} %take.8), channel_id=1, source_target_pairs={{0,2},{1,3},{2,4},{3,5},{4,6},{5,7},{6,0},{7,1},{8,10},{9,11},{10,... | collective-permute-start | bytes 589832 | tf_op jit(solution)/shard_map/cond/branch_0_fun/ppermute | solution.py:262
  22.2 7.7 %collective-permute-start.6 = (bf16[32,3072]{1,0:T(8,128)(2,1)S(1)}, bf16[32,3072]{1,0:T(8,128)(2,1)S(1)}, u32[]{:S(2)}, u32[]{:S(2)}) collective-permute-start(bf16[32,3072]{1,0:T(8,128)(2,1)S(1)} %take.9), channel_id=1, source_target_pairs={{0,6},{1,7},{2,0},{3,1},{4,2},{5,3},{6,4},{7,5},{8,14},{9,15},{10,... | collective-permute-start | bytes 589832 | tf_op jit(solution)/shard_map/cond/branch_0_fun/ppermute | solution.py:262
  30.0 29.5 %copy-start.1 = (bf16[1,1,2,512,512]{4,3,2,1,0:T(8,128)(2,1)S(1)}, bf16[1,1,2,512,512]{4,3,2,1,0:T(8,128)(2,1)}, u32[]{:S(2)}) copy-start(bf16[1,1,2,512,512]{4,3,2,1,0:T(8,128)(2,1)} %param.12) | copy-start | bytes 3145732
  30.0 29.5 %copy-start.2 = (bf16[1,1,2,512,512]{4,3,2,1,0:T(8,128)(2,1)S(1)}, bf16[1,1,2,512,512]{4,3,2,1,0:T(8,128)(2,1)}, u32[]{:S(2)}) copy-start(bf16[1,1,2,512,512]{4,3,2,1,0:T(8,128)(2,1)} %param.13) | copy-start | bytes 3145732
  62.4 22.8 %all-to-all-start.1 = ((bf16[32,32,512]{2,1,0:T(8,128)(2,1)}), bf16[32,32,512]{2,1,0:T(8,128)(2,1)S(1)}, u32[]{:S(2)}, u32[]{:S(2)}) async-start(bf16[32,32,512]{2,1,0:T(8,128)(2,1)} %precondition.1), calls=%async_computation.1 | async-start | bytes 2097152 | tf_op jit(solution)/shard_map/all_to_all | solution.py:280
  66.8 3.9 %copy-start.3 = (f32[1,1,2,512,512]{4,3,2,1,0:T(8,128)S(1)}, f32[1,1,2,512,512]{4,3,2,1,0:T(8,128)}, u32[]{:S(2)}) copy-start(f32[1,1,2,512,512]{4,3,2,1,0:T(8,128)} %param.10) | copy-start | bytes 6291460

commit v6 on v5

--- a/solution.py
+++ b/solution.py
@@ -10,6 +10,8 @@
 BETA = 0.9
 EPS = 1e-06
 Y_ORDER = (2, 1, 3)
+PRE_PARTS = 2
+CUTS = (0, 512)
 VMEM_LIMIT = 24 * 1024 * 1024
 ANY = pl.BlockSpec(memory_space=pl.ANY)
 HBM = pl.BlockSpec(memory_space=pltpu.HBM)
@@ -173,18 +175,28 @@
     )(owners, *parts, *after)
 
 
-def precondition_kernel(g_ref, l_ref, r_ref, out_ref):
+def precondition_kernel(g_ref, l_ref, r_ref, out_ref, held, sems):
     slots, block, _ = l_ref.shape
     rows = g_ref.shape[0] // slots
+    part = rows // PRE_PARTS
+    lines = block // PRE_PARTS
+    copies = []
     for b in range(slots):
         g = g_ref[b * rows : (b + 1) * rows].reshape(block, block)
         half = jnp.dot(l_ref[b], g, preferred_element_type=jnp.float32).astype(jnp.bfloat16)
         pre = jnp.dot(half, r_ref[b], preferred_element_type=jnp.float32)
         gfull = g.astype(jnp.float32)
         scale = jnp.sqrt(jnp.mean(gfull * gfull)) / jnp.sqrt(jnp.mean(pre * pre) + EPS)
-        out_ref[b * rows : (b + 1) * rows] = (
-            (scale * pre).astype(jnp.bfloat16).reshape(rows, *g_ref.shape[1:])
-        )
+        for i in range(PRE_PARTS):
+            scaled = scale * pre[i * lines : (i + 1) * lines]
+            place = slice(b * rows + i * part, b * rows + (i + 1) * part)
+            held[place] = scaled.astype(jnp.bfloat16).reshape(part, *g_ref.shape[1:])
+            copies.append(
+                pltpu.make_async_copy(held.at[place], out_ref.at[place], sems.at[len(copies)])
+            )
+            copies[-1].start()
+    for copy in copies:
+        copy.wait()
 
 
 def precondition(incoming, lroots, rroots):
@@ -193,7 +205,11 @@
         precondition_kernel,
         out_shape=jax.ShapeDtypeStruct(incoming.shape, jnp.bfloat16),
         in_specs=[VMEM] * 3,
-        out_specs=VMEM,
+        out_specs=ANY,
+        scratch_shapes=[
+            pltpu.VMEM(incoming.shape, jnp.bfloat16),
+            pltpu.SemaphoreType.DMA((slots * PRE_PARTS,)),
+        ],
         compiler_params=params(),
         cost_estimate=pl.CostEstimate(
             flops=4 * slots * block**3, bytes_accessed=8 * slots * block**2, transcendentals=0
@@ -264,16 +280,14 @@
     def directly(parts):
         return add_up([parts[0]] + [send_y(parts[step], step) for step in Y_ORDER], block)
 
-    def round_ring(parts):
-        running = take(parts[0], 0, block)
-        for part in parts[:0:-1]:
-            running = plus(part, send_y(running, 1))
-        running = send_y(running, 1)
-        rest = [take(part, block, width, running) for part in parts]
-        rest = add_up([rest[0]] + [send_y(rest[step], step) for step in Y_ORDER], block)
-        return join([running, rest])
-
-    total = lax.cond(rep_index % 2 == 0, directly, round_ring, parts)
+    def in_turns(parts):
+        done = []
+        for start, stop in zip(CUTS, [*CUTS[1:], width], strict=True):
+            some = [take(part, start, stop, *done[-1:]) for part in parts]
+            done.append(add_up([some[0]] + [send_y(some[step], step) for step in Y_ORDER], block))
+        return join(done)
+
+    total = lax.cond(rep_index % 2 == 1, directly, in_turns, parts)
     outgoing = fill_slots([total], owners, n_fsdp, block)
     incoming = lax.all_to_all(outgoing, "fsdp", split_axis=0, concat_axis=0, tiled=True)
     results = precondition(incoming, left_root[0, 0], right_root[0, 0])

time: 86.7 us -> 85.4 us (0.985)
  the two profiles are of different devices: /device:TPU:33 before, /device:TPU:32 now
where the time goes in v6:
time: 85.4 us; the launch traced here: 83.8 us
  blocking collectives  30 us (35%)
  waiting for transfers between devices  22.7 us (27%)
  starting transfers between devices  16.7 us (20%)
  Pallas kernels  7.5 us (9%)
  matrix products  5.95 us (7%)
    all_to_all x1, blocking collectives, on_device(): lax.all_to_all(outgoing, 'fsdp', split_axis=0, concat_axis=0, tiled=True)  30 us
    all_to_all x1, waiting for transfers between devices, on_device(): lax.all_to_all(results, 'fsdp', split_axis=0, concat_axis=0, tiled=True)  13.7 us
    ppermute x6, starting transfers between devices, send_y(): lax.ppermute(array, 'rep', [(i, (i + 2 * step) % n_rep) for i in range(n_...  10.8 us
    ppermute x6, waiting for transfers between devices, send_y(): lax.ppermute(array, 'rep', [(i, (i + 2 * step) % n_rep) for i in range(n_...  8.02 us
    all_to_all x1, starting transfers between devices, on_device(): lax.all_to_all(results, 'fsdp', split_axis=0, concat_axis=0, tiled=True)  5.79 us
    dot_general x1, matrix products, statistics(): lax.dot_general(g, g, (((0,), (0,)), ((), ())), preferred_element_type=jn...  3.88 us
    pallas_call x2, Pallas kernels, groups(): pl.pallas_call(functools.partial(groups_kernel, ring, width, other), out_...  2.67 us
    pallas_call x1, Pallas kernels, precondition(): pl.pallas_call(precondition_kernel, out_shape=jax.ShapeDtypeStruct(incomi...  2.63 us
  transfers between devices with their start and end apart: 8, of which 8 were waited for; matrix products, arithmetic and copies ran while one was open for 7% of the time, Pallas kernels for 2%

profile of v6, /device:TPU:32, one launch (start us, length us, event | category | flops | bytes accessed | tf_op | source)
XLA Modules:
  0.0 83.8 jit_solution(11714647750183198348)
XLA Ops:
  0.6 0.0 copy-start
  0.6 1.3 %groups.3 = bf16[4,32,3584]{2,1,0:T(8,128)(2,1)S(1)} custom-call(bf16[32,28672]{1,0:T(8,128)(2,1)} %bitcast.26), custom_call_target="tpu_custom_call" | custom-call | flops 1 | bytes 2097152 | tf_op jit(solution)/shard_map/groups/pallas_call | solution.py:48
  2.0 0.1 collective-permute-start.9
  2.1 1.3 %groups.2.kept = bf16[4,32,3584]{2,1,0:T(8,128)(2,1)S(1)} custom-call(bf16[32,28672]{1,0:T(8,128)(2,1)} %bitcast.27), custom_call_target="tpu_custom_call" | custom-call | flops 1 | bytes 2097152 | tf_op jit(solution)/shard_map/groups/pallas_call | solution.py:48
  3.5 0.0 copy-done
  3.5 0.1 dynamic-slice_bitcast_fusion.owners
  3.5 1.0 %collective-permute-done.9.other = bf16[4,32,3584]{2,1,0:T(8,128)(2,1)S(1)} collective-permute-done((bf16[4,32,3584]{2,1,0:T(8,128)(2,1)S(1)}, bf16[4,32,3584]{2,1,0:T(8,128)(2,1)S(1)}, u32[]{:S(2)}, u32[]{:S(2)}) %collective-permute-start.9) | collective-permute-done | bytes 917536 | tf_op jit(solution)/shard_map/ppermute | solution.py:274
  4.5 0.1 pair_sum.1
  4.6 19.1 %conditional.1 = (bf16[32,3584]{1,0:T(8,128)(2,1)S(1)}) conditional(s32[]{:T(128)} %convert_element_type.3, (bf16[32,3584]{1,0:T(8,128)(2,1)S(1)}, bf16[32,3584]{1,0:T(8,128)(2,1)S(1)}, bf16[32,3584]{1,0:T(8,128)(2,1)S(1)}, bf16[32,3584]{1,0:T(8,128)(2,1)S(1)}) %tuple.14, (bf16[32,3584]{1,0:T(8,128)(2,1)S(1)}, bf16[32,3584]{1,0:T(8,128)(2,1)S(1)}, ...), branch_computations={%region_0.1_spmd, %region_1.2_spmd} | conditional | flops 11 | bytes 2752771 | solution.py:290
  4.7 3.1 %collective-permute-start.2 = (bf16[32,512]{1,0:T(8,128)(2,1)S(1)}, bf16[32,512]{1,0:T(8,128)(2,1)S(1)}, u32[]{:S(2)}, u32[]{:S(2)}) collective-permute-start(bf16[32,512]{1,0:T(8,128)(2,1)S(1)} %take.11), channel_id=1, source_target_pairs={{0,6},{1,7},{2,0},{3,1},{4,2},{5,3},{6,4},{7,5},{8,14},{9,15},{10,... | collective-permute-start | bytes 98312 | tf_op jit(solution)/shard_map/cond/branch_0_fun/ppermute | solution.py:278
  7.8 0.0 collective-permute-start.1
  7.8 2.2 %collective-permute-start = (bf16[32,512]{1,0:T(8,128)(2,1)S(1)}, bf16[32,512]{1,0:T(8,128)(2,1)S(1)}, u32[]{:S(2)}, u32[]{:S(2)}) collective-permute-start(bf16[32,512]{1,0:T(8,128)(2,1)S(1)} %take.9), channel_id=1, source_target_pairs={{0,4},{1,5},{2,6},{3,7},{4,0},{5,1},{6,2},{7,3},{8,12},{9,13},{10,... | collective-permute-start | bytes 98312 | tf_op jit(solution)/shard_map/cond/branch_0_fun/ppermute | solution.py:278
  10.0 1.2 %collective-permute-done.2.refs_3_ = bf16[32,512]{1,0:T(8,128)(2,1)S(1)} collective-permute-done((bf16[32,512]{1,0:T(8,128)(2,1)S(1)}, bf16[32,512]{1,0:T(8,128)(2,1)S(1)}, u32[]{:S(2)}, u32[]{:S(2)}) %collective-permute-start.2) | collective-permute-done | bytes 32800 | tf_op jit(solution)/shard_map/cond/branch_0_fun/ppermute | solution.py:278
  11.2 2.2 %collective-permute-done.1.refs_2_ = bf16[32,512]{1,0:T(8,128)(2,1)S(1)} collective-permute-done((bf16[32,512]{1,0:T(8,128)(2,1)S(1)}, bf16[32,512]{1,0:T(8,128)(2,1)S(1)}, u32[]{:S(2)}, u32[]{:S(2)}) %collective-permute-start.1) | collective-permute-done | bytes 32800 | tf_op jit(solution)/shard_map/cond/branch_0_fun/ppermute | solution.py:278
  13.5 0.2 collective-permute-done.refs_1_
  13.8 2.2 %collective-permute-start.3 = (bf16[32,3072]{1,0:T(8,128)(2,1)S(1)}, bf16[32,3072]{1,0:T(8,128)(2,1)S(1)}, u32[]{:S(2)}, u32[]{:S(2)}) collective-permute-start(bf16[32,3072]{1,0:T(8,128)(2,1)S(1)} %take.13), channel_id=1, source_target_pairs={{0,4},{1,5},{2,6},{3,7},{4,0},{5,1},{6,2},{7,3},{8,12},{9,13},{10,... | collective-permute-start | bytes 589832 | tf_op jit(solution)/shard_map/cond/branch_0_fun/ppermute | solution.py:278
  16.0 1.9 %collective-permute-start.4 = (bf16[32,3072]{1,0:T(8,128)(2,1)S(1)}, bf16[32,3072]{1,0:T(8,128)(2,1)S(1)}, u32[]{:S(2)}, u32[]{:S(2)}) collective-permute-start(bf16[32,3072]{1,0:T(8,128)(2,1)S(1)} %take.14), channel_id=1, source_target_pairs={{0,2},{1,3},{2,4},{3,5},{4,6},{5,7},{6,0},{7,1},{8,10},{9,11},{10,... | collective-permute-start | bytes 589832 | tf_op jit(solution)/shard_map/cond/branch_0_fun/ppermute | solution.py:278
  17.9 1.4 %collective-permute-start.5 = (bf16[32,3072]{1,0:T(8,128)(2,1)S(1)}, bf16[32,3072]{1,0:T(8,128)(2,1)S(1)}, u32[]{:S(2)}, u32[]{:S(2)}) collective-permute-start(bf16[32,3072]{1,0:T(8,128)(2,1)S(1)} %take.15), channel_id=1, source_target_pairs={{0,6},{1,7},{2,0},{3,1},{4,2},{5,3},{6,4},{7,5},{8,14},{9,15},{10,... | collective-permute-start | bytes 589832 | tf_op jit(solution)/shard_map/cond/branch_0_fun/ppermute | solution.py:278
  19.3 1.7 %collective-permute-done.3.refs_1_ = bf16[32,3072]{1,0:T(8,128)(2,1)S(1)} collective-permute-done((bf16[32,3072]{1,0:T(8,128)(2,1)S(1)}, bf16[32,3072]{1,0:T(8,128)(2,1)S(1)}, u32[]{:S(2)}, u32[]{:S(2)}) %collective-permute-start.3) | collective-permute-done | bytes 196640 | tf_op jit(solution)/shard_map/cond/branch_0_fun/ppermute | solution.py:278
  21.1 2.1 %collective-permute-done.4.refs_2_ = bf16[32,3072]{1,0:T(8,128)(2,1)S(1)} collective-permute-done((bf16[32,3072]{1,0:T(8,128)(2,1)S(1)}, bf16[32,3072]{1,0:T(8,128)(2,1)S(1)}, u32[]{:S(2)}, u32[]{:S(2)}) %collective-permute-start.4) | collective-permute-done | bytes 196640 | tf_op jit(solution)/shard_map/cond/branch_0_fun/ppermute | solution.py:278
  23.1 0.5 collective-permute-done.5.refs_3_
  23.6 0.1 add_up.4.refs_1_
  23.8 0.0 copy-start.1
  23.8 0.0 copy-start.2
  23.8 0.6 fill_slots.1
  24.4 30.0 %all_to_all.10.g_ref = bf16[32,32,512]{2,1,0:T(8,128)(2,1)S(1)} all-to-all(bf16[32,32,512]{2,1,0:T(8,128)(2,1)S(1)} %fill_slots.1), channel_id=1, replica_groups=mesh['fsdp'=32,'rep'=8] {'fsdp'}, dimensions={0} | all-to-all | bytes 2097152 | tf_op jit(solution)/shard_map/all_to_all | solution.py:292
  54.5 0.0 copy-done.1
  54.5 0.0 copy-done.2
  54.5 2.6 %precondition.1 = bf16[32,32,512]{2,1,0:T(8,128)(2,1)} custom-call(bf16[32,32,512]{2,1,0:T(8,128)(2,1)S(1)} %all_to_all.10.g_ref, bf16[2,512,512]{2,1,0:T(8,128)(2,1)S(1)} %bitcast.24, bf16[2,512,512]{2,1,0:T(8,128)(2,1)S(1)} %bitcast.25), custom_call_target="tpu_custom_call" | custom-call | flops 1073741824 | bytes 4194304 | tf_op jit(solution)/shard_map/precondition/pallas_call | solution.py:204
  57.1 5.8 %all-to-all-start.1 = ((bf16[32,32,512]{2,1,0:T(8,128)(2,1)}), bf16[32,32,512]{2,1,0:T(8,128)(2,1)S(1)}, u32[]{:S(2)}, u32[]{:S(2)}) async-start(bf16[32,32,512]{2,1,0:T(8,128)(2,1)} %precondition.1), calls=%async_computation.1 | async-start | bytes 2097152 | tf_op jit(solution)/shard_map/all_to_all | solution.py:294
  62.9 0.0 copy-start.3
  62.9 3.9 %fusion = f32[1,1,2,512,512]{4,3,2,1,0:T(8,128)} fusion(f32[1,1,2,512,512]{4,3,2,1,0:T(8,128)} %param.11, bf16[2,512,512]{2,1,0:T(8,128)(2,1)S(1)} %bitcast.22), kind=kOutput, calls=%fused_computation.1 | convolution fusion | flops 538443776 | bytes 5242880 | tf_op jit(solution)/shard_map/vmap()/dot_general | solution.py:253
  66.8 0.0 copy-done.3
  66.8 2.1 %fusion.1 = f32[1,1,2,512,512]{4,3,2,1,0:T(8,128)} fusion(f32[1,1,2,512,512]{4,3,2,1,0:T(8,128)S(1)} %copy-done.3, bf16[2,512,512]{2,1,0:T(8,128)(2,1)S(1)} %bitcast.23), kind=kOutput, calls=%fused_computation.3 | convolution fusion | flops 538443776 | bytes 5242880 | tf_op jit(solution)/shard_map/vmap()/dot_general | solution.py:250
  68.9 13.7 %all-to-all-done.1.returned = bf16[32,32,512]{2,1,0:T(8,128)(2,1)S(1)} async-done(((bf16[32,32,512]{2,1,0:T(8,128)(2,1)}), bf16[32,32,512]{2,1,0:T(8,128)(2,1)S(1)}, u32[]{:S(2)}, u32[]{:S(2)}) %all-to-all-start.1) | async-done | bytes 1048608 | tf_op jit(solution)/shard_map/all_to_all | solution.py:294
  82.6 1.3 %collect.1 = bf16[32,3584]{1,0:T(8,128)(2,1)} custom-call(s32[7]{0:T(128)S(1)} %dynamic-slice_bitcast_fusion.owners, bf16[32,32,512]{2,1,0:T(8,128)(2,1)S(1)} %all-to-all-done.1.returned), custom_call_target="tpu_custom_call" | custom-call | tf_op jit(solution)/shard_map/collect/pallas_call | solution.py:236
  (10 shorter events, 0.1 us)
Async XLA Ops:
  0.6 2.8 %copy-start = (s32[2,56]{1,0:T(2,128)S(1)}, s32[2,56]{1,0:T(2,128)}, u32[]{:S(2)}) copy-start(s32[2,56]{1,0:T(2,128)} %param.9) | copy-start | bytes 1348
  2.0 2.6 %collective-permute-start.9 = (bf16[4,32,3584]{2,1,0:T(8,128)(2,1)S(1)}, bf16[4,32,3584]{2,1,0:T(8,128)(2,1)S(1)}, u32[]{:S(2)}, u32[]{:S(2)}) collective-permute-start(bf16[4,32,3584]{2,1,0:T(8,128)(2,1)S(1)} %groups.3), channel_id=1, source_target_pairs={{0,1},{1,0},{2,3},{3,2},{4,5},{5,4},{6,7},{7,6},{8,9},{9,8},{10,11... | collective-permute-start | bytes 2752520 | tf_op jit(solution)/shard_map/ppermute | solution.py:274
  4.7 6.5 %collective-permute-start.2 = (bf16[32,512]{1,0:T(8,128)(2,1)S(1)}, bf16[32,512]{1,0:T(8,128)(2,1)S(1)}, u32[]{:S(2)}, u32[]{:S(2)}) collective-permute-start(bf16[32,512]{1,0:T(8,128)(2,1)S(1)} %take.11), channel_id=1, source_target_pairs={{0,6},{1,7},{2,0},{3,1},{4,2},{5,3},{6,4},{7,5},{8,14},{9,15},{10,... | collective-permute-start | bytes 98312 | tf_op jit(solution)/shard_map/cond/branch_0_fun/ppermute | solution.py:278
  7.8 5.7 %collective-permute-start.1 = (bf16[32,512]{1,0:T(8,128)(2,1)S(1)}, bf16[32,512]{1,0:T(8,128)(2,1)S(1)}, u32[]{:S(2)}, u32[]{:S(2)}) collective-permute-start(bf16[32,512]{1,0:T(8,128)(2,1)S(1)} %take.10), channel_id=1, source_target_pairs={{0,2},{1,3},{2,4},{3,5},{4,6},{5,7},{6,0},{7,1},{8,10},{9,11},{10,... | collective-permute-start | bytes 98312 | tf_op jit(solution)/shard_map/cond/branch_0_fun/ppermute | solution.py:278
  7.8 5.9 %collective-permute-start = (bf16[32,512]{1,0:T(8,128)(2,1)S(1)}, bf16[32,512]{1,0:T(8,128)(2,1)S(1)}, u32[]{:S(2)}, u32[]{:S(2)}) collective-permute-start(bf16[32,512]{1,0:T(8,128)(2,1)S(1)} %take.9), channel_id=1, source_target_pairs={{0,4},{1,5},{2,6},{3,7},{4,0},{5,1},{6,2},{7,3},{8,12},{9,13},{10,... | collective-permute-start | bytes 98312 | tf_op jit(solution)/shard_map/cond/branch_0_fun/ppermute | solution.py:278
  13.8 7.3 %collective-permute-start.3 = (bf16[32,3072]{1,0:T(8,128)(2,1)S(1)}, bf16[32,3072]{1,0:T(8,128)(2,1)S(1)}, u32[]{:S(2)}, u32[]{:S(2)}) collective-permute-start(bf16[32,3072]{1,0:T(8,128)(2,1)S(1)} %take.13), channel_id=1, source_target_pairs={{0,4},{1,5},{2,6},{3,7},{4,0},{5,1},{6,2},{7,3},{8,12},{9,13},{10,... | collective-permute-start | bytes 589832 | tf_op jit(solution)/shard_map/cond/branch_0_fun/ppermute | solution.py:278
  16.0 7.2 %collective-permute-start.4 = (bf16[32,3072]{1,0:T(8,128)(2,1)S(1)}, bf16[32,3072]{1,0:T(8,128)(2,1)S(1)}, u32[]{:S(2)}, u32[]{:S(2)}) collective-permute-start(bf16[32,3072]{1,0:T(8,128)(2,1)S(1)} %take.14), channel_id=1, source_target_pairs={{0,2},{1,3},{2,4},{3,5},{4,6},{5,7},{6,0},{7,1},{8,10},{9,11},{10,... | collective-permute-start | bytes 589832 | tf_op jit(solution)/shard_map/cond/branch_0_fun/ppermute | solution.py:278
  17.9 5.7 %collective-permute-start.5 = (bf16[32,3072]{1,0:T(8,128)(2,1)S(1)}, bf16[32,3072]{1,0:T(8,128)(2,1)S(1)}, u32[]{:S(2)}, u32[]{:S(2)}) collective-permute-start(bf16[32,3072]{1,0:T(8,128)(2,1)S(1)} %take.15), channel_id=1, source_target_pairs={{0,6},{1,7},{2,0},{3,1},{4,2},{5,3},{6,4},{7,5},{8,14},{9,15},{10,... | collective-permute-start | bytes 589832 | tf_op jit(solution)/shard_map/cond/branch_0_fun/ppermute | solution.py:278
  23.8 30.7 %copy-start.1 = (bf16[1,1,2,512,512]{4,3,2,1,0:T(8,128)(2,1)S(1)}, bf16[1,1,2,512,512]{4,3,2,1,0:T(8,128)(2,1)}, u32[]{:S(2)}) copy-start(bf16[1,1,2,512,512]{4,3,2,1,0:T(8,128)(2,1)} %param.12) | copy-start | bytes 3145732
  23.8 30.7 %copy-start.2 = (bf16[1,1,2,512,512]{4,3,2,1,0:T(8,128)(2,1)S(1)}, bf16[1,1,2,512,512]{4,3,2,1,0:T(8,128)(2,1)}, u32[]{:S(2)}) copy-start(bf16[1,1,2,512,512]{4,3,2,1,0:T(8,128)(2,1)} %param.13) | copy-start | bytes 3145732
  57.1 25.5 %all-to-all-start.1 = ((bf16[32,32,512]{2,1,0:T(8,128)(2,1)}), bf16[32,32,512]{2,1,0:T(8,128)(2,1)S(1)}, u32[]{:S(2)}, u32[]{:S(2)}) async-start(bf16[32,32,512]{2,1,0:T(8,128)(2,1)} %precondition.1), calls=%async_computation.1 | async-start | bytes 2097152 | tf_op jit(solution)/shard_map/all_to_all | solution.py:294
  62.9 3.9 %copy-start.3 = (f32[1,1,2,512,512]{4,3,2,1,0:T(8,128)S(1)}, f32[1,1,2,512,512]{4,3,2,1,0:T(8,128)}, u32[]{:S(2)}) copy-start(f32[1,1,2,512,512]{4,3,2,1,0:T(8,128)} %param.10) | copy-start | bytes 6291460

commit v7 on v6

--- a/solution.py
+++ b/solution.py
@@ -12,6 +12,7 @@
 Y_ORDER = (2, 1, 3)
 PRE_PARTS = 2
 CUTS = (0, 512)
+TURNS = ((2, 1), (3,))
 VMEM_LIMIT = 24 * 1024 * 1024
 ANY = pl.BlockSpec(memory_space=pl.ANY)
 HBM = pl.BlockSpec(memory_space=pltpu.HBM)
@@ -281,10 +282,14 @@
         return add_up([parts[0]] + [send_y(parts[step], step) for step in Y_ORDER], block)
 
     def in_turns(parts):
-        done = []
+        done, after = [], []
         for start, stop in zip(CUTS, [*CUTS[1:], width], strict=True):
-            some = [take(part, start, stop, *done[-1:]) for part in parts]
-            done.append(add_up([some[0]] + [send_y(some[step], step) for step in Y_ORDER], block))
+            terms = [take(parts[0], start, stop)]
+            for turn in TURNS if start == 0 else (Y_ORDER,):
+                some = [take(parts[step], start, stop, *after) for step in turn]
+                terms += [send_y(part, step) for part, step in zip(some, turn, strict=True)]
+                after = terms[-1:]
+            done.append(add_up(terms, block))
         return join(done)
 
     total = lax.cond(rep_index % 2 == 1, directly, in_turns, parts)

time: 85.4 us -> 84.4 us (0.988); the launches traced: 83.8 us -> 84.2 us
  waiting for transfers between devices: 22.7 us -> 26.6 us
  starting transfers between devices: 16.7 us -> 13 us
    ppermute x6, waiting for transfers between devices: 8.02 us -> 12.7 us  [send_y(): lax.ppermute(array, 'rep', [(i, (i + 2 * step) % n_rep) for i in range(n_...]
    ppermute x6, starting transfers between devices: 10.8 us -> 8.01 us  [send_y(): lax.ppermute(array, 'rep', [(i, (i + 2 * step) % n_rep) for i in range(n_...]
    all_to_all x1, starting transfers between devices: 5.79 us -> 4.91 us  [on_device(): lax.all_to_all(results, 'fsdp', split_axis=0, concat_axis=0, tiled=True)]
  transfers between devices with their start and end apart: 8 -> 8, of which waited for: 8 -> 5; matrix products, arithmetic and copies ran while one was open for 7% -> 7% of each run, Pallas kernels for 2% -> 2%
where the time goes in v7:
time: 84.4 us; the launch traced here: 84.2 us
  blocking collectives  30.1 us (36%)
  waiting for transfers between devices  26.6 us (32%)
  starting transfers between devices  13 us (15%)
  Pallas kernels  7.5 us (9%)
  matrix products  5.96 us (7%)
    all_to_all x1, blocking collectives, on_device(): lax.all_to_all(outgoing, 'fsdp', split_axis=0, concat_axis=0, tiled=True)  30.1 us
    all_to_all x1, waiting for transfers between devices, on_device(): lax.all_to_all(results, 'fsdp', split_axis=0, concat_axis=0, tiled=True)  12.9 us
    ppermute x6, waiting for transfers between devices, send_y(): lax.ppermute(array, 'rep', [(i, (i + 2 * step) % n_rep) for i in range(n_...  12.7 us
    ppermute x6, starting transfers between devices, send_y(): lax.ppermute(array, 'rep', [(i, (i + 2 * step) % n_rep) for i in range(n_...  8.01 us
    all_to_all x1, starting transfers between devices, on_device(): lax.all_to_all(results, 'fsdp', split_axis=0, concat_axis=0, tiled=True)  4.91 us
    dot_general x1, matrix products, statistics(): lax.dot_general(g, g, (((0,), (0,)), ((), ())), preferred_element_type=jn...  3.88 us
    pallas_call x2, Pallas kernels, groups(): pl.pallas_call(functools.partial(groups_kernel, ring, width, other), out_...  2.67 us
    pallas_call x1, Pallas kernels, precondition(): pl.pallas_call(precondition_kernel, out_shape=jax.ShapeDtypeStruct(incomi...  2.63 us
  transfers between devices with their start and end apart: 8, of which 5 were waited for; matrix products, arithmetic and copies ran while one was open for 7% of the time, Pallas kernels for 2%

profile of v7, /device:TPU:32, one launch (start us, length us, event | category | flops | bytes accessed | tf_op | source)
XLA Modules:
  0.0 84.2 jit_solution(13736525865394887480)
XLA Ops:
  0.6 0.0 copy-start
  0.6 1.3 %groups.3 = bf16[4,32,3584]{2,1,0:T(8,128)(2,1)S(1)} custom-call(bf16[32,28672]{1,0:T(8,128)(2,1)} %bitcast.26), custom_call_target="tpu_custom_call" | custom-call | flops 1 | bytes 2097152 | tf_op jit(solution)/shard_map/groups/pallas_call | solution.py:49
  2.0 0.1 collective-permute-start.9
  2.1 1.3 %groups.2.kept = bf16[4,32,3584]{2,1,0:T(8,128)(2,1)S(1)} custom-call(bf16[32,28672]{1,0:T(8,128)(2,1)} %bitcast.27), custom_call_target="tpu_custom_call" | custom-call | flops 1 | bytes 2097152 | tf_op jit(solution)/shard_map/groups/pallas_call | solution.py:49
  3.5 0.0 copy-done
  3.5 0.1 dynamic-slice_bitcast_fusion.owners
  3.5 1.0 %collective-permute-done.9.other = bf16[4,32,3584]{2,1,0:T(8,128)(2,1)S(1)} collective-permute-done((bf16[4,32,3584]{2,1,0:T(8,128)(2,1)S(1)}, bf16[4,32,3584]{2,1,0:T(8,128)(2,1)S(1)}, u32[]{:S(2)}, u32[]{:S(2)}) %collective-permute-start.9) | collective-permute-done | bytes 917536 | tf_op jit(solution)/shard_map/ppermute | solution.py:275
  4.5 0.1 pair_sum.1
  4.6 21.0 %conditional.1 = (bf16[32,3584]{1,0:T(8,128)(2,1)S(1)}) conditional(s32[]{:T(128)} %convert_element_type.3, (bf16[32,3584]{1,0:T(8,128)(2,1)S(1)}, bf16[32,3584]{1,0:T(8,128)(2,1)S(1)}, bf16[32,3584]{1,0:T(8,128)(2,1)S(1)}, bf16[32,3584]{1,0:T(8,128)(2,1)S(1)}) %tuple.14, (bf16[32,3584]{1,0:T(8,128)(2,1)S(1)}, bf16[32,3584]{1,0:T(8,128)(2,1)S(1)}, ...), branch_computations={%region_0.1_spmd, %region_1.2_spmd} | conditional | flops 11 | bytes 2752771 | solution.py:295
  4.7 1.7 %collective-permute-start.1 = (bf16[32,512]{1,0:T(8,128)(2,1)S(1)}, bf16[32,512]{1,0:T(8,128)(2,1)S(1)}, u32[]{:S(2)}, u32[]{:S(2)}) collective-permute-start(bf16[32,512]{1,0:T(8,128)(2,1)S(1)} %take.10), channel_id=1, source_target_pairs={{0,2},{1,3},{2,4},{3,5},{4,6},{5,7},{6,0},{7,1},{8,10},{9,11},{10,... | collective-permute-start | bytes 98312 | tf_op jit(solution)/shard_map/cond/branch_0_fun/ppermute | solution.py:279
  6.3 5.2 %collective-permute-done.1.refs_0_.refs_2_ = bf16[32,512]{1,0:T(8,128)(2,1)S(1)} collective-permute-done((bf16[32,512]{1,0:T(8,128)(2,1)S(1)}, bf16[32,512]{1,0:T(8,128)(2,1)S(1)}, u32[]{:S(2)}, u32[]{:S(2)}) %collective-permute-start.1) | collective-permute-done | bytes 32800 | tf_op jit(solution)/shard_map/cond/branch_0_fun/ppermute | solution.py:279
  11.5 0.6 collective-permute-start.2
  12.1 3.4 %collective-permute-done.2.refs_3_.refs_0_ = bf16[32,512]{1,0:T(8,128)(2,1)S(1)} collective-permute-done((bf16[32,512]{1,0:T(8,128)(2,1)S(1)}, bf16[32,512]{1,0:T(8,128)(2,1)S(1)}, u32[]{:S(2)}, u32[]{:S(2)}) %collective-permute-start.2) | collective-permute-done | bytes 32800 | tf_op jit(solution)/shard_map/cond/branch_0_fun/ppermute | solution.py:279
  15.5 1.1 %collective-permute-start.3 = (bf16[32,3072]{1,0:T(8,128)(2,1)S(1)}, bf16[32,3072]{1,0:T(8,128)(2,1)S(1)}, u32[]{:S(2)}, u32[]{:S(2)}) collective-permute-start(bf16[32,3072]{1,0:T(8,128)(2,1)S(1)} %take.13), channel_id=1, source_target_pairs={{0,4},{1,5},{2,6},{3,7},{4,0},{5,1},{6,2},{7,3},{8,12},{9,13},{10,... | collective-permute-start | bytes 589832 | tf_op jit(solution)/shard_map/cond/branch_0_fun/ppermute | solution.py:279
  16.6 1.8 %collective-permute-start.4 = (bf16[32,3072]{1,0:T(8,128)(2,1)S(1)}, bf16[32,3072]{1,0:T(8,128)(2,1)S(1)}, u32[]{:S(2)}, u32[]{:S(2)}) collective-permute-start(bf16[32,3072]{1,0:T(8,128)(2,1)S(1)} %take.14), channel_id=1, source_target_pairs={{0,2},{1,3},{2,4},{3,5},{4,6},{5,7},{6,0},{7,1},{8,10},{9,11},{10,... | collective-permute-start | bytes 589832 | tf_op jit(solution)/shard_map/cond/branch_0_fun/ppermute | solution.py:279
  18.4 1.6 %collective-permute-start.5 = (bf16[32,3072]{1,0:T(8,128)(2,1)S(1)}, bf16[32,3072]{1,0:T(8,128)(2,1)S(1)}, u32[]{:S(2)}, u32[]{:S(2)}) collective-permute-start(bf16[32,3072]{1,0:T(8,128)(2,1)S(1)} %take.15), channel_id=1, source_target_pairs={{0,6},{1,7},{2,0},{3,1},{4,2},{5,3},{6,4},{7,5},{8,14},{9,15},{10,... | collective-permute-start | bytes 589832 | tf_op jit(solution)/shard_map/cond/branch_0_fun/ppermute | solution.py:279
  20.0 1.3 %collective-permute-start = (bf16[32,512]{1,0:T(8,128)(2,1)S(1)}, bf16[32,512]{1,0:T(8,128)(2,1)S(1)}, u32[]{:S(2)}, u32[]{:S(2)}) collective-permute-start(bf16[32,512]{1,0:T(8,128)(2,1)S(1)} %take.9), channel_id=1, source_target_pairs={{0,4},{1,5},{2,6},{3,7},{4,0},{5,1},{6,2},{7,3},{8,12},{9,13},{10,... | collective-permute-start | bytes 98312 | tf_op jit(solution)/shard_map/cond/branch_0_fun/ppermute | solution.py:279
  21.3 4.1 %collective-permute-done.refs_1_ = bf16[32,512]{1,0:T(8,128)(2,1)S(1)} collective-permute-done((bf16[32,512]{1,0:T(8,128)(2,1)S(1)}, bf16[32,512]{1,0:T(8,128)(2,1)S(1)}, u32[]{:S(2)}, u32[]{:S(2)}) %collective-permute-start) | collective-permute-done | bytes 32800 | tf_op jit(solution)/shard_map/cond/branch_0_fun/ppermute | solution.py:279
  25.5 0.0 collective-permute-done.3.refs_1_
  25.5 0.0 collective-permute-done.4.refs_2_
  25.5 0.0 collective-permute-done.5.refs_3_
  25.5 0.1 add_up.4.refs_1_
  25.6 0.0 copy-start.1
  25.6 0.0 copy-start.2
  25.7 0.6 fill_slots.1
  26.3 30.1 %all_to_all.10.g_ref = bf16[32,32,512]{2,1,0:T(8,128)(2,1)S(1)} all-to-all(bf16[32,32,512]{2,1,0:T(8,128)(2,1)S(1)} %fill_slots.1), channel_id=1, replica_groups=mesh['fsdp'=32,'rep'=8] {'fsdp'}, dimensions={0} | all-to-all | bytes 2097152 | tf_op jit(solution)/shard_map/all_to_all | solution.py:297
  56.4 0.0 copy-done.1
  56.4 0.0 copy-done.2
  56.4 2.6 %precondition.1 = bf16[32,32,512]{2,1,0:T(8,128)(2,1)} custom-call(bf16[32,32,512]{2,1,0:T(8,128)(2,1)S(1)} %all_to_all.10.g_ref, bf16[2,512,512]{2,1,0:T(8,128)(2,1)S(1)} %bitcast.24, bf16[2,512,512]{2,1,0:T(8,128)(2,1)S(1)} %bitcast.25), custom_call_target="tpu_custom_call" | custom-call | flops 1073741824 | bytes 4194304 | tf_op jit(solution)/shard_map/precondition/pallas_call | solution.py:205
  59.1 4.9 %all-to-all-start.1 = ((bf16[32,32,512]{2,1,0:T(8,128)(2,1)}), bf16[32,32,512]{2,1,0:T(8,128)(2,1)S(1)}, u32[]{:S(2)}, u32[]{:S(2)}) async-start(bf16[32,32,512]{2,1,0:T(8,128)(2,1)} %precondition.1), calls=%async_computation.1 | async-start | bytes 2097152 | tf_op jit(solution)/shard_map/all_to_all | solution.py:299
  64.0 0.0 copy-start.3
  64.0 3.9 %fusion = f32[1,1,2,512,512]{4,3,2,1,0:T(8,128)} fusion(f32[1,1,2,512,512]{4,3,2,1,0:T(8,128)} %param.11, bf16[2,512,512]{2,1,0:T(8,128)(2,1)S(1)} %bitcast.22), kind=kOutput, calls=%fused_computation.1 | convolution fusion | flops 538443776 | bytes 5242880 | tf_op jit(solution)/shard_map/vmap()/dot_general | solution.py:254
  67.9 0.0 copy-done.3
  67.9 2.1 %fusion.1 = f32[1,1,2,512,512]{4,3,2,1,0:T(8,128)} fusion(f32[1,1,2,512,512]{4,3,2,1,0:T(8,128)S(1)} %copy-done.3, bf16[2,512,512]{2,1,0:T(8,128)(2,1)S(1)} %bitcast.23), kind=kOutput, calls=%fused_computation.3 | convolution fusion | flops 538443776 | bytes 5242880 | tf_op jit(solution)/shard_map/vmap()/dot_general | solution.py:251
  70.0 12.9 %all-to-all-done.1.returned = bf16[32,32,512]{2,1,0:T(8,128)(2,1)S(1)} async-done(((bf16[32,32,512]{2,1,0:T(8,128)(2,1)}), bf16[32,32,512]{2,1,0:T(8,128)(2,1)S(1)}, u32[]{:S(2)}, u32[]{:S(2)}) %all-to-all-start.1) | async-done | bytes 1048608 | tf_op jit(solution)/shard_map/all_to_all | solution.py:299
  82.9 1.3 %collect.1 = bf16[32,3584]{1,0:T(8,128)(2,1)} custom-call(s32[7]{0:T(128)S(1)} %dynamic-slice_bitcast_fusion.owners, bf16[32,32,512]{2,1,0:T(8,128)(2,1)S(1)} %all-to-all-done.1.returned), custom_call_target="tpu_custom_call" | custom-call | tf_op jit(solution)/shard_map/collect/pallas_call | solution.py:237
  (10 shorter events, 0.1 us)
Async XLA Ops:
  0.6 2.8 %copy-start = (s32[2,56]{1,0:T(2,128)S(1)}, s32[2,56]{1,0:T(2,128)}, u32[]{:S(2)}) copy-start(s32[2,56]{1,0:T(2,128)} %param.9) | copy-start | bytes 1348
  2.0 2.6 %collective-permute-start.9 = (bf16[4,32,3584]{2,1,0:T(8,128)(2,1)S(1)}, bf16[4,32,3584]{2,1,0:T(8,128)(2,1)S(1)}, u32[]{:S(2)}, u32[]{:S(2)}) collective-permute-start(bf16[4,32,3584]{2,1,0:T(8,128)(2,1)S(1)} %groups.3), channel_id=1, source_target_pairs={{0,1},{1,0},{2,3},{3,2},{4,5},{5,4},{6,7},{7,6},{8,9},{9,8},{10,11... | collective-permute-start | bytes 2752520 | tf_op jit(solution)/shard_map/ppermute | solution.py:275
  4.7 6.9 %collective-permute-start.1 = (bf16[32,512]{1,0:T(8,128)(2,1)S(1)}, bf16[32,512]{1,0:T(8,128)(2,1)S(1)}, u32[]{:S(2)}, u32[]{:S(2)}) collective-permute-start(bf16[32,512]{1,0:T(8,128)(2,1)S(1)} %take.10), channel_id=1, source_target_pairs={{0,2},{1,3},{2,4},{3,5},{4,6},{5,7},{6,0},{7,1},{8,10},{9,11},{10,... | collective-permute-start | bytes 98312 | tf_op jit(solution)/shard_map/cond/branch_0_fun/ppermute | solution.py:279
  11.5 3.9 %collective-permute-start.2 = (bf16[32,512]{1,0:T(8,128)(2,1)S(1)}, bf16[32,512]{1,0:T(8,128)(2,1)S(1)}, u32[]{:S(2)}, u32[]{:S(2)}) collective-permute-start(bf16[32,512]{1,0:T(8,128)(2,1)S(1)} %take.11), channel_id=1, source_target_pairs={{0,6},{1,7},{2,0},{3,1},{4,2},{5,3},{6,4},{7,5},{8,14},{9,15},{10,... | collective-permute-start | bytes 98312 | tf_op jit(solution)/shard_map/cond/branch_0_fun/ppermute | solution.py:279
  15.5 10.0 %collective-permute-start.3 = (bf16[32,3072]{1,0:T(8,128)(2,1)S(1)}, bf16[32,3072]{1,0:T(8,128)(2,1)S(1)}, u32[]{:S(2)}, u32[]{:S(2)}) collective-permute-start(bf16[32,3072]{1,0:T(8,128)(2,1)S(1)} %take.13), channel_id=1, source_target_pairs={{0,4},{1,5},{2,6},{3,7},{4,0},{5,1},{6,2},{7,3},{8,12},{9,13},{10,... | collective-permute-start | bytes 589832 | tf_op jit(solution)/shard_map/cond/branch_0_fun/ppermute | solution.py:279
  16.6 8.9 %collective-permute-start.4 = (bf16[32,3072]{1,0:T(8,128)(2,1)S(1)}, bf16[32,3072]{1,0:T(8,128)(2,1)S(1)}, u32[]{:S(2)}, u32[]{:S(2)}) collective-permute-start(bf16[32,3072]{1,0:T(8,128)(2,1)S(1)} %take.14), channel_id=1, source_target_pairs={{0,2},{1,3},{2,4},{3,5},{4,6},{5,7},{6,0},{7,1},{8,10},{9,11},{10,... | collective-permute-start | bytes 589832 | tf_op jit(solution)/shard_map/cond/branch_0_fun/ppermute | solution.py:279
  18.4 7.0 %collective-permute-start.5 = (bf16[32,3072]{1,0:T(8,128)(2,1)S(1)}, bf16[32,3072]{1,0:T(8,128)(2,1)S(1)}, u32[]{:S(2)}, u32[]{:S(2)}) collective-permute-start(bf16[32,3072]{1,0:T(8,128)(2,1)S(1)} %take.15), channel_id=1, source_target_pairs={{0,6},{1,7},{2,0},{3,1},{4,2},{5,3},{6,4},{7,5},{8,14},{9,15},{10,... | collective-permute-start | bytes 589832 | tf_op jit(solution)/shard_map/cond/branch_0_fun/ppermute | solution.py:279
  20.0 5.4 %collective-permute-start = (bf16[32,512]{1,0:T(8,128)(2,1)S(1)}, bf16[32,512]{1,0:T(8,128)(2,1)S(1)}, u32[]{:S(2)}, u32[]{:S(2)}) collective-permute-start(bf16[32,512]{1,0:T(8,128)(2,1)S(1)} %take.9), channel_id=1, source_target_pairs={{0,4},{1,5},{2,6},{3,7},{4,0},{5,1},{6,2},{7,3},{8,12},{9,13},{10,... | collective-permute-start | bytes 98312 | tf_op jit(solution)/shard_map/cond/branch_0_fun/ppermute | solution.py:279
  25.6 30.8 %copy-start.1 = (bf16[1,1,2,512,512]{4,3,2,1,0:T(8,128)(2,1)S(1)}, bf16[1,1,2,512,512]{4,3,2,1,0:T(8,128)(2,1)}, u32[]{:S(2)}) copy-start(bf16[1,1,2,512,512]{4,3,2,1,0:T(8,128)(2,1)} %param.12) | copy-start | bytes 3145732
  25.6 30.8 %copy-start.2 = (bf16[1,1,2,512,512]{4,3,2,1,0:T(8,128)(2,1)S(1)}, bf16[1,1,2,512,512]{4,3,2,1,0:T(8,128)(2,1)}, u32[]{:S(2)}) copy-start(bf16[1,1,2,512,512]{4,3,2,1,0:T(8,128)(2,1)} %param.13) | copy-start | bytes 3145732
  59.1 23.8 %all-to-all-start.1 = ((bf16[32,32,512]{2,1,0:T(8,128)(2,1)}), bf16[32,32,512]{2,1,0:T(8,128)(2,1)S(1)}, u32[]{:S(2)}, u32[]{:S(2)}) async-start(bf16[32,32,512]{2,1,0:T(8,128)(2,1)} %precondition.1), calls=%async_computation.1 | async-start | bytes 2097152 | tf_op jit(solution)/shard_map/all_to_all | solution.py:299
  64.0 3.9 %copy-start.3 = (f32[1,1,2,512,512]{4,3,2,1,0:T(8,128)S(1)}, f32[1,1,2,512,512]{4,3,2,1,0:T(8,128)}, u32[]{:S(2)}) copy-start(f32[1,1,2,512,512]{4,3,2,1,0:T(8,128)} %param.10) | copy-start | bytes 6291460

commit v8 on v7

--- a/solution.py
+++ b/solution.py
@@ -11,7 +11,8 @@
 EPS = 1e-06
 Y_ORDER = (2, 1, 3)
 PRE_PARTS = 2
-CUTS = (0, 512)
+CUTS = (0, 256)
+STEP = 256
 TURNS = ((2, 1), (3,))
 VMEM_LIMIT = 24 * 1024 * 1024
 ANY = pl.BlockSpec(memory_space=pl.ANY)
@@ -279,7 +280,7 @@
         return lax.ppermute(array, "rep", [(i, (i + 2 * step) % n_rep) for i in range(n_rep)])
 
     def directly(parts):
-        return add_up([parts[0]] + [send_y(parts[step], step) for step in Y_ORDER], block)
+        return add_up([parts[0]] + [send_y(parts[step], step) for step in Y_ORDER], STEP)
 
     def in_turns(parts):
         done, after = [], []
@@ -289,7 +290,7 @@
                 some = [take(parts[step], start, stop, *after) for step in turn]
                 terms += [send_y(part, step) for part, step in zip(some, turn, strict=True)]
                 after = terms[-1:]
-            done.append(add_up(terms, block))
+            done.append(add_up(terms, STEP))
         return join(done)
 
     total = lax.cond(rep_index % 2 == 1, directly, in_turns, parts)

time: 84.4 us -> 83.9 us (level)
  no operation moved by 1% of the time
where the time goes in v8:
time: 83.9 us; the launch traced here: 83.6 us
  blocking collectives  30.5 us (36%)
  waiting for transfers between devices  26.1 us (31%)
  starting transfers between devices  12.6 us (15%)
  Pallas kernels  7.5 us (9%)
  matrix products  5.95 us (7%)
    all_to_all x1, blocking collectives, on_device(): lax.all_to_all(outgoing, 'fsdp', split_axis=0, concat_axis=0, tiled=True)  30.5 us
    all_to_all x1, waiting for transfers between devices, on_device(): lax.all_to_all(results, 'fsdp', split_axis=0, concat_axis=0, tiled=True)  13 us
    ppermute x6, waiting for transfers between devices, send_y(): lax.ppermute(array, 'rep', [(i, (i + 2 * step) % n_rep) for i in range(n_...  12.1 us
    ppermute x6, starting transfers between devices, send_y(): lax.ppermute(array, 'rep', [(i, (i + 2 * step) % n_rep) for i in range(n_...  8.01 us
    all_to_all x1, starting transfers between devices, on_device(): lax.all_to_all(results, 'fsdp', split_axis=0, concat_axis=0, tiled=True)  4.48 us
    dot_general x1, matrix products, statistics(): lax.dot_general(g, g, (((0,), (0,)), ((), ())), preferred_element_type=jn...  3.88 us
    pallas_call x2, Pallas kernels, groups(): pl.pallas_call(functools.partial(groups_kernel, ring, width, other), out_...  2.67 us
    pallas_call x1, Pallas kernels, precondition(): pl.pallas_call(precondition_kernel, out_shape=jax.ShapeDtypeStruct(incomi...  2.63 us
  transfers between devices with their start and end apart: 8, of which 5 were waited for; matrix products, arithmetic and copies ran while one was open for 7% of the time, Pallas kernels for 2%

profile of v8, /device:TPU:32, one launch (start us, length us, event | category | flops | bytes accessed | tf_op | source)
XLA Modules:
  0.0 83.6 jit_solution(4607825223905451901)
XLA Ops:
  0.6 0.0 copy-start
  0.6 1.3 %groups.3 = bf16[4,32,3584]{2,1,0:T(8,128)(2,1)S(1)} custom-call(bf16[32,28672]{1,0:T(8,128)(2,1)} %bitcast.26), custom_call_target="tpu_custom_call" | custom-call | flops 1 | bytes 2097152 | tf_op jit(solution)/shard_map/groups/pallas_call | solution.py:50
  2.0 0.1 collective-permute-start.9
  2.1 1.3 %groups.2.kept = bf16[4,32,3584]{2,1,0:T(8,128)(2,1)S(1)} custom-call(bf16[32,28672]{1,0:T(8,128)(2,1)} %bitcast.27), custom_call_target="tpu_custom_call" | custom-call | flops 1 | bytes 2097152 | tf_op jit(solution)/shard_map/groups/pallas_call | solution.py:50
  3.5 0.0 copy-done
  3.5 0.1 dynamic-slice_bitcast_fusion.owners
  3.5 1.0 %collective-permute-done.9.other = bf16[4,32,3584]{2,1,0:T(8,128)(2,1)S(1)} collective-permute-done((bf16[4,32,3584]{2,1,0:T(8,128)(2,1)S(1)}, bf16[4,32,3584]{2,1,0:T(8,128)(2,1)S(1)}, u32[]{:S(2)}, u32[]{:S(2)}) %collective-permute-start.9) | collective-permute-done | bytes 917536 | tf_op jit(solution)/shard_map/ppermute | solution.py:276
  4.5 0.1 pair_sum.1
  4.6 20.4 %conditional.1 = (bf16[32,3584]{1,0:T(8,128)(2,1)S(1)}) conditional(s32[]{:T(128)} %convert_element_type.3, (bf16[32,3584]{1,0:T(8,128)(2,1)S(1)}, bf16[32,3584]{1,0:T(8,128)(2,1)S(1)}, bf16[32,3584]{1,0:T(8,128)(2,1)S(1)}, bf16[32,3584]{1,0:T(8,128)(2,1)S(1)}) %tuple.14, (bf16[32,3584]{1,0:T(8,128)(2,1)S(1)}, bf16[32,3584]{1,0:T(8,128)(2,1)S(1)}, ...), branch_computations={%region_0.1_spmd, %region_1.2_spmd} | conditional | flops 11 | bytes 2752771 | solution.py:296
  4.7 1.7 %collective-permute-start.1 = (bf16[32,256]{1,0:T(8,128)(2,1)S(1)}, bf16[32,256]{1,0:T(8,128)(2,1)S(1)}, u32[]{:S(2)}, u32[]{:S(2)}) collective-permute-start(bf16[32,256]{1,0:T(8,128)(2,1)S(1)} %take.10), channel_id=1, source_target_pairs={{0,2},{1,3},{2,4},{3,5},{4,6},{5,7},{6,0},{7,1},{8,10},{9,11},{10,... | collective-permute-start | bytes 49160 | tf_op jit(solution)/shard_map/cond/branch_0_fun/ppermute | solution.py:280
  6.3 4.9 %collective-permute-done.1.refs_0_.refs_2_ = bf16[32,256]{1,0:T(8,128)(2,1)S(1)} collective-permute-done((bf16[32,256]{1,0:T(8,128)(2,1)S(1)}, bf16[32,256]{1,0:T(8,128)(2,1)S(1)}, u32[]{:S(2)}, u32[]{:S(2)}) %collective-permute-start.1) | collective-permute-done | bytes 16416 | tf_op jit(solution)/shard_map/cond/branch_0_fun/ppermute | solution.py:280
  11.2 0.6 collective-permute-start.2
  11.7 3.2 %collective-permute-done.2.refs_3_.refs_0_ = bf16[32,256]{1,0:T(8,128)(2,1)S(1)} collective-permute-done((bf16[32,256]{1,0:T(8,128)(2,1)S(1)}, bf16[32,256]{1,0:T(8,128)(2,1)S(1)}, u32[]{:S(2)}, u32[]{:S(2)}) %collective-permute-start.2) | collective-permute-done | bytes 16416 | tf_op jit(solution)/shard_map/cond/branch_0_fun/ppermute | solution.py:280
  14.9 1.0 %collective-permute-start.3 = (bf16[32,3328]{1,0:T(8,128)(2,1)S(1)}, bf16[32,3328]{1,0:T(8,128)(2,1)S(1)}, u32[]{:S(2)}, u32[]{:S(2)}) collective-permute-start(bf16[32,3328]{1,0:T(8,128)(2,1)S(1)} %take.13), channel_id=1, source_target_pairs={{0,4},{1,5},{2,6},{3,7},{4,0},{5,1},{6,2},{7,3},{8,12},{9,13},{10,... | collective-permute-start | bytes 638984 | tf_op jit(solution)/shard_map/cond/branch_0_fun/ppermute | solution.py:280
  16.0 2.0 %collective-permute-start.4 = (bf16[32,3328]{1,0:T(8,128)(2,1)S(1)}, bf16[32,3328]{1,0:T(8,128)(2,1)S(1)}, u32[]{:S(2)}, u32[]{:S(2)}) collective-permute-start(bf16[32,3328]{1,0:T(8,128)(2,1)S(1)} %take.14), channel_id=1, source_target_pairs={{0,2},{1,3},{2,4},{3,5},{4,6},{5,7},{6,0},{7,1},{8,10},{9,11},{10,... | collective-permute-start | bytes 638984 | tf_op jit(solution)/shard_map/cond/branch_0_fun/ppermute | solution.py:280
  18.0 1.4 %collective-permute-start.5 = (bf16[32,3328]{1,0:T(8,128)(2,1)S(1)}, bf16[32,3328]{1,0:T(8,128)(2,1)S(1)}, u32[]{:S(2)}, u32[]{:S(2)}) collective-permute-start(bf16[32,3328]{1,0:T(8,128)(2,1)S(1)} %take.15), channel_id=1, source_target_pairs={{0,6},{1,7},{2,0},{3,1},{4,2},{5,3},{6,4},{7,5},{8,14},{9,15},{10,... | collective-permute-start | bytes 638984 | tf_op jit(solution)/shard_map/cond/branch_0_fun/ppermute | solution.py:280
  19.4 1.4 %collective-permute-start = (bf16[32,256]{1,0:T(8,128)(2,1)S(1)}, bf16[32,256]{1,0:T(8,128)(2,1)S(1)}, u32[]{:S(2)}, u32[]{:S(2)}) collective-permute-start(bf16[32,256]{1,0:T(8,128)(2,1)S(1)} %take.9), channel_id=1, source_target_pairs={{0,4},{1,5},{2,6},{3,7},{4,0},{5,1},{6,2},{7,3},{8,12},{9,13},{10,... | collective-permute-start | bytes 49160 | tf_op jit(solution)/shard_map/cond/branch_0_fun/ppermute | solution.py:280
  20.8 4.0 %collective-permute-done.refs_1_ = bf16[32,256]{1,0:T(8,128)(2,1)S(1)} collective-permute-done((bf16[32,256]{1,0:T(8,128)(2,1)S(1)}, bf16[32,256]{1,0:T(8,128)(2,1)S(1)}, u32[]{:S(2)}, u32[]{:S(2)}) %collective-permute-start) | collective-permute-done | bytes 16416 | tf_op jit(solution)/shard_map/cond/branch_0_fun/ppermute | solution.py:280
  24.9 0.0 collective-permute-done.3.refs_1_
  24.9 0.0 collective-permute-done.4.refs_2_
  24.9 0.0 collective-permute-done.5.refs_3_
  24.9 0.1 add_up.4.refs_1_
  25.0 0.0 copy-start.1
  25.1 0.0 copy-start.2
  25.1 0.6 fill_slots.1
  25.7 30.5 %all_to_all.10.g_ref = bf16[32,32,512]{2,1,0:T(8,128)(2,1)S(1)} all-to-all(bf16[32,32,512]{2,1,0:T(8,128)(2,1)S(1)} %fill_slots.1), channel_id=1, replica_groups=mesh['fsdp'=32,'rep'=8] {'fsdp'}, dimensions={0} | all-to-all | bytes 2097152 | tf_op jit(solution)/shard_map/all_to_all | solution.py:298
  56.2 0.0 copy-done.1
  56.2 0.0 copy-done.2
  56.2 2.6 %precondition.1 = bf16[32,32,512]{2,1,0:T(8,128)(2,1)} custom-call(bf16[32,32,512]{2,1,0:T(8,128)(2,1)S(1)} %all_to_all.10.g_ref, bf16[2,512,512]{2,1,0:T(8,128)(2,1)S(1)} %bitcast.24, bf16[2,512,512]{2,1,0:T(8,128)(2,1)S(1)} %bitcast.25), custom_call_target="tpu_custom_call" | custom-call | flops 1073741824 | bytes 4194304 | tf_op jit(solution)/shard_map/precondition/pallas_call | solution.py:206
  58.8 4.5 %all-to-all-start.1 = ((bf16[32,32,512]{2,1,0:T(8,128)(2,1)}), bf16[32,32,512]{2,1,0:T(8,128)(2,1)S(1)}, u32[]{:S(2)}, u32[]{:S(2)}) async-start(bf16[32,32,512]{2,1,0:T(8,128)(2,1)} %precondition.1), calls=%async_computation.1 | async-start | bytes 2097152 | tf_op jit(solution)/shard_map/all_to_all | solution.py:300
  63.3 0.0 copy-start.3
  63.3 3.9 %fusion = f32[1,1,2,512,512]{4,3,2,1,0:T(8,128)} fusion(f32[1,1,2,512,512]{4,3,2,1,0:T(8,128)} %param.11, bf16[2,512,512]{2,1,0:T(8,128)(2,1)S(1)} %bitcast.22), kind=kOutput, calls=%fused_computation.1 | convolution fusion | flops 538443776 | bytes 5242880 | tf_op jit(solution)/shard_map/vmap()/dot_general | solution.py:255
  67.2 0.0 copy-done.3
  67.2 2.1 %fusion.1 = f32[1,1,2,512,512]{4,3,2,1,0:T(8,128)} fusion(f32[1,1,2,512,512]{4,3,2,1,0:T(8,128)S(1)} %copy-done.3, bf16[2,512,512]{2,1,0:T(8,128)(2,1)S(1)} %bitcast.23), kind=kOutput, calls=%fused_computation.3 | convolution fusion | flops 538443776 | bytes 5242880 | tf_op jit(solution)/shard_map/vmap()/dot_general | solution.py:252
  69.3 13.0 %all-to-all-done.1.returned = bf16[32,32,512]{2,1,0:T(8,128)(2,1)S(1)} async-done(((bf16[32,32,512]{2,1,0:T(8,128)(2,1)}), bf16[32,32,512]{2,1,0:T(8,128)(2,1)S(1)}, u32[]{:S(2)}, u32[]{:S(2)}) %all-to-all-start.1) | async-done | bytes 1048608 | tf_op jit(solution)/shard_map/all_to_all | solution.py:300
  82.3 1.3 %collect.1 = bf16[32,3584]{1,0:T(8,128)(2,1)} custom-call(s32[7]{0:T(128)S(1)} %dynamic-slice_bitcast_fusion.owners, bf16[32,32,512]{2,1,0:T(8,128)(2,1)S(1)} %all-to-all-done.1.returned), custom_call_target="tpu_custom_call" | custom-call | tf_op jit(solution)/shard_map/collect/pallas_call | solution.py:238
  (10 shorter events, 0.1 us)
Async XLA Ops:
  0.6 2.8 %copy-start = (s32[2,56]{1,0:T(2,128)S(1)}, s32[2,56]{1,0:T(2,128)}, u32[]{:S(2)}) copy-start(s32[2,56]{1,0:T(2,128)} %param.9) | copy-start | bytes 1348
  2.0 2.6 %collective-permute-start.9 = (bf16[4,32,3584]{2,1,0:T(8,128)(2,1)S(1)}, bf16[4,32,3584]{2,1,0:T(8,128)(2,1)S(1)}, u32[]{:S(2)}, u32[]{:S(2)}) collective-permute-start(bf16[4,32,3584]{2,1,0:T(8,128)(2,1)S(1)} %groups.3), channel_id=1, source_target_pairs={{0,1},{1,0},{2,3},{3,2},{4,5},{5,4},{6,7},{7,6},{8,9},{9,8},{10,11... | collective-permute-start | bytes 2752520 | tf_op jit(solution)/shard_map/ppermute | solution.py:276
  4.7 6.5 %collective-permute-start.1 = (bf16[32,256]{1,0:T(8,128)(2,1)S(1)}, bf16[32,256]{1,0:T(8,128)(2,1)S(1)}, u32[]{:S(2)}, u32[]{:S(2)}) collective-permute-start(bf16[32,256]{1,0:T(8,128)(2,1)S(1)} %take.10), channel_id=1, source_target_pairs={{0,2},{1,3},{2,4},{3,5},{4,6},{5,7},{6,0},{7,1},{8,10},{9,11},{10,... | collective-permute-start | bytes 49160 | tf_op jit(solution)/shard_map/cond/branch_0_fun/ppermute | solution.py:280
  11.2 3.7 %collective-permute-start.2 = (bf16[32,256]{1,0:T(8,128)(2,1)S(1)}, bf16[32,256]{1,0:T(8,128)(2,1)S(1)}, u32[]{:S(2)}, u32[]{:S(2)}) collective-permute-start(bf16[32,256]{1,0:T(8,128)(2,1)S(1)} %take.11), channel_id=1, source_target_pairs={{0,6},{1,7},{2,0},{3,1},{4,2},{5,3},{6,4},{7,5},{8,14},{9,15},{10,... | collective-permute-start | bytes 49160 | tf_op jit(solution)/shard_map/cond/branch_0_fun/ppermute | solution.py:280
  14.9 9.9 %collective-permute-start.3 = (bf16[32,3328]{1,0:T(8,128)(2,1)S(1)}, bf16[32,3328]{1,0:T(8,128)(2,1)S(1)}, u32[]{:S(2)}, u32[]{:S(2)}) collective-permute-start(bf16[32,3328]{1,0:T(8,128)(2,1)S(1)} %take.13), channel_id=1, source_target_pairs={{0,4},{1,5},{2,6},{3,7},{4,0},{5,1},{6,2},{7,3},{8,12},{9,13},{10,... | collective-permute-start | bytes 638984 | tf_op jit(solution)/shard_map/cond/branch_0_fun/ppermute | solution.py:280
  16.0 8.9 %collective-permute-start.4 = (bf16[32,3328]{1,0:T(8,128)(2,1)S(1)}, bf16[32,3328]{1,0:T(8,128)(2,1)S(1)}, u32[]{:S(2)}, u32[]{:S(2)}) collective-permute-start(bf16[32,3328]{1,0:T(8,128)(2,1)S(1)} %take.14), channel_id=1, source_target_pairs={{0,2},{1,3},{2,4},{3,5},{4,6},{5,7},{6,0},{7,1},{8,10},{9,11},{10,... | collective-permute-start | bytes 638984 | tf_op jit(solution)/shard_map/cond/branch_0_fun/ppermute | solution.py:280
  18.0 6.9 %collective-permute-start.5 = (bf16[32,3328]{1,0:T(8,128)(2,1)S(1)}, bf16[32,3328]{1,0:T(8,128)(2,1)S(1)}, u32[]{:S(2)}, u32[]{:S(2)}) collective-permute-start(bf16[32,3328]{1,0:T(8,128)(2,1)S(1)} %take.15), channel_id=1, source_target_pairs={{0,6},{1,7},{2,0},{3,1},{4,2},{5,3},{6,4},{7,5},{8,14},{9,15},{10,... | collective-permute-start | bytes 638984 | tf_op jit(solution)/shard_map/cond/branch_0_fun/ppermute | solution.py:280
  19.4 5.5 %collective-permute-start = (bf16[32,256]{1,0:T(8,128)(2,1)S(1)}, bf16[32,256]{1,0:T(8,128)(2,1)S(1)}, u32[]{:S(2)}, u32[]{:S(2)}) collective-permute-start(bf16[32,256]{1,0:T(8,128)(2,1)S(1)} %take.9), channel_id=1, source_target_pairs={{0,4},{1,5},{2,6},{3,7},{4,0},{5,1},{6,2},{7,3},{8,12},{9,13},{10,... | collective-permute-start | bytes 49160 | tf_op jit(solution)/shard_map/cond/branch_0_fun/ppermute | solution.py:280
  25.0 31.2 %copy-start.1 = (bf16[1,1,2,512,512]{4,3,2,1,0:T(8,128)(2,1)S(1)}, bf16[1,1,2,512,512]{4,3,2,1,0:T(8,128)(2,1)}, u32[]{:S(2)}) copy-start(bf16[1,1,2,512,512]{4,3,2,1,0:T(8,128)(2,1)} %param.12) | copy-start | bytes 3145732
  25.1 31.1 %copy-start.2 = (bf16[1,1,2,512,512]{4,3,2,1,0:T(8,128)(2,1)S(1)}, bf16[1,1,2,512,512]{4,3,2,1,0:T(8,128)(2,1)}, u32[]{:S(2)}) copy-start(bf16[1,1,2,512,512]{4,3,2,1,0:T(8,128)(2,1)} %param.13) | copy-start | bytes 3145732
  58.8 23.5 %all-to-all-start.1 = ((bf16[32,32,512]{2,1,0:T(8,128)(2,1)}), bf16[32,32,512]{2,1,0:T(8,128)(2,1)S(1)}, u32[]{:S(2)}, u32[]{:S(2)}) async-start(bf16[32,32,512]{2,1,0:T(8,128)(2,1)} %precondition.1), calls=%async_computation.1 | async-start | bytes 2097152 | tf_op jit(solution)/shard_map/all_to_all | solution.py:300
  63.3 3.9 %copy-start.3 = (f32[1,1,2,512,512]{4,3,2,1,0:T(8,128)S(1)}, f32[1,1,2,512,512]{4,3,2,1,0:T(8,128)}, u32[]{:S(2)}) copy-start(f32[1,1,2,512,512]{4,3,2,1,0:T(8,128)} %param.10) | copy-start | bytes 6291460
